TPU v7x, 128 devices: a whole 4x4x4 slice. The times are simulated.
128 devices in a mesh: ch: 16 (over x, y), sx: 4 (over z), sy: 2 (over core).
Axes of the slice: x: 4, y: 4, z: 4, core: 2. Of those that a mesh axis runs over, the one named last changes fastest.
Arguments:
- volume: bfloat16 [512, 2, 16, 256], P('ch', None, 'sx', 'sy'), may hold values from -6 to 6
- kernel: bfloat16 [27, 512, 512], P(None, 'ch'), may hold values from -0.0546875 to 0.0546875
- cotangent: bfloat16 [512, 2, 16, 256], P('ch', None, 'sx', 'sy'), may hold values from -6 to 6
Outputs:
- response: bfloat16 [512, 2, 16, 256], P('ch', None, 'sx', 'sy')
- volume_grad: bfloat16 [512, 2, 16, 256], P('ch', None, 'sx', 'sy')
- kernel_grad: float32 [27, 512, 512], P(None, 'ch')
All inputs are finite; a program needn't handle non-finite values.
Results may differ from a plain program's by a relative error of at most 0.001.
Values may be sent and summed in bfloat16 or wider, within the bound.
A program may use at most 128 MiB of HBM per device.

v0:
```python
import jax
import jax.numpy as jnp
from jax import lax
from jax.sharding import PartitionSpec as P


def with_halo(cells, sides, width):
    for axis, dim in sides:
        count = lax.axis_size(axis)
        ends = count - 1
        head = lax.slice_in_dim(cells, 0, width, axis=dim)
        tail = lax.slice_in_dim(cells, cells.shape[dim] - width, cells.shape[dim], axis=dim)
        cells = jnp.concatenate(
            [
                lax.ppermute(tail, axis, [(i, (i + 1) % count) for i in range(ends)]),
                cells,
                lax.ppermute(head, axis, [((i + 1) % count, i) for i in range(ends)]),
            ],
            axis=dim,
        )
    return cells


def pad_depth(field):
    return jnp.pad(field, ((0, 0), (1, 1), (0, 0), (0, 0)))


def tap_group(padded, layer, depth, wide, tall):
    pieces = [
        padded[:, layer : layer + depth, step_x : step_x + wide, step_y : step_y + tall]
        for step_x in range(3)
        for step_y in range(3)
    ]
    return jnp.concatenate(pieces, axis=0)


def shards(volume, kernel, cotangent):
    chans = volume.shape[0]
    depth = volume.shape[1]
    wide = volume.shape[2]
    tall = volume.shape[3]
    out_all = kernel.shape[2]
    out_local = cotangent.shape[0]
    rimmed = with_halo(volume, (("sx", 2), ("sy", 3)), 1)
    padded_in = pad_depth(rimmed)
    groups = [tap_group(padded_in, layer, depth, wide, tall) for layer in range(3)]
    total = jnp.zeros((out_local * lax.axis_size("ch"), depth, wide, tall), jnp.float32)
    for partial_layer in range(3):
        slab = kernel[9 * partial_layer : 9 * partial_layer + 9]
        slab = slab.reshape(9 * chans, out_local * lax.axis_size("ch"))
        total = total + jnp.einsum(
            "ko,kzxy->ozxy", slab, groups[partial_layer], preferred_element_type=jnp.float32
        )
    response = lax.psum_scatter(total, "ch", scatter_dimension=0, tiled=True).astype(jnp.bfloat16)
    grad_full = lax.all_gather(cotangent, "ch", axis=0, tiled=True)
    grad_rimmed = with_halo(grad_full, (("sx", 2), ("sy", 3)), 1)
    padded_grad = pad_depth(grad_rimmed)
    back_sum = jnp.zeros((chans, depth, wide, tall), jnp.float32)
    for step_z in range(3):
        for step_x in range(3):
            for step_y in range(3):
                tap = step_z * 9 + step_x * 3 + step_y
                window = padded_grad[
                    :,
                    2 - step_z : 2 - step_z + depth,
                    2 - step_x : 2 - step_x + wide,
                    2 - step_y : 2 - step_y + tall,
                ]
                back_sum = back_sum + jnp.einsum(
                    "io,ozxy->izxy", kernel[tap], window, preferred_element_type=jnp.float32
                )
    blocks = []
    for layer in range(3):
        block = jnp.einsum(
            "kzxy,ozxy->ko", groups[layer], grad_full, preferred_element_type=jnp.float32
        )
        blocks.append(block.reshape(9, chans, out_all))
    local_grad = jnp.concatenate(blocks, axis=0)
    cells = depth * wide * tall * lax.axis_size("sx") * lax.axis_size("sy")
    scale = 1.0 / jnp.sqrt(jnp.float32(cells))
    kernel_grad = lax.psum(local_grad, ("sx", "sy")) * scale
    return (response, back_sum.astype(jnp.bfloat16), kernel_grad)


def solution(mesh):
    in_specs = (P("ch", None, "sx", "sy"), P(None, "ch", None), P("ch", None, "sx", "sy"))
    out_specs = (P("ch", None, "sx", "sy"), P("ch", None, "sx", "sy"), P(None, "ch", None))
    return jax.shard_map(shards, mesh=mesh, in_specs=in_specs, out_specs=out_specs, check_vma=False)
```

profile of v0, /device:TPU:1, one launch (start us, length us, event | category | flops | bytes accessed | tf_op | source)
XLA Modules:
  0.0 210.8 jit_solution(171439667334088170)
XLA Ops:
  7.2 0.9 copy.21
  8.1 4.4 %collective-permute-start = (bf16[32,2,1,128]{3,0,2,1:T(8,128)(2,1)S(1)}, bf16[32,2,1,128]{3,0,2,1:T(8,128)(2,1)S(1)}, u32[]{:S(2)}, u32[]{:S(2)}) collective-permute-start(bf16[32,2,1,128]{3,0,2,1:T(8,128)(2,1)S(1)} %get-tuple-element.35), channel_id=1, source_target_pairs={{0,2},{2,4},{4,6},{1,3},{3,5},{5,7},{8,10},{10,12},{12,14},{9,11},... | collective-permute-start | bytes 49160 | tf_op jit(solution)/shard_map/ppermute | solution.py:15
  12.5 1.5 copy.28
  14.1 1.3 collective-permute-start.1
  15.4 0.9 constant_dynamic-update-slice_fusion.1
  16.2 2.5 %collective-permute-done.1 = bf16[32,2,1,128]{3,0,2,1:T(8,128)(2,1)S(1)} collective-permute-done((bf16[32,2,1,128]{3,0,2,1:T(8,128)(2,1)S(1)}, bf16[32,2,1,128]{3,0,2,1:T(8,128)(2,1)S(1)}, u32[]{:S(2)}, u32[]{:S(2)}) %collective-permute-start.1) | collective-permute-done | bytes 16416 | tf_op jit(solution)/shard_map/ppermute | solution.py:17
  18.8 1.3 collective-permute-start.2
  20.1 1.2 fusion.157
  21.4 0.6 dynamic-slice
  22.6 3.8 %collective-permute-start.3 = (bf16[32,2,6,1]{3,0,2,1:T(8,128)(2,1)S(1)}, bf16[32,2,6,1]{3,0,2,1:T(8,128)(2,1)S(1)}, u32[]{:S(2)}, u32[]{:S(2)}) collective-permute-start(bf16[32,2,6,1]{3,0,2,1:T(8,128)(2,1)S(1)} %get-tuple-element.33), channel_id=1, source_target_pairs={{1,0},{3,2},{5,4},{7,6},{9,8},{11,10},{13,12},{15,14},{17,16},{19,... | collective-permute-start | bytes 2312 | tf_op jit(solution)/shard_map/ppermute | solution.py:17
  26.6 0.8 collective-permute-done.3
  28.9 0.7 fusion.161
  30.0 0.7 fusion.160
  30.8 0.7 add_bitcast_fusion
  31.5 1.9 copy.27
  33.4 82.8 %all-reduce.7 = bf16[512,2,4,128]{3,2,1,0:T(4,128)(2,1)S(1)} all-reduce(f32[512,2,4,128]{3,2,1,0:T(4,128)} %copy.27), channel_id=2, replica_groups=mesh['ch'=16,'sx'=4,'sy'=2] {'ch'}, use_global_device_ids=true, to_apply=%region_0.1.clone | all-reduce | flops 524288 | bytes 3145728
  116.2 0.7 dynamic-slice_convert_fusion
  116.8 1.9 fusion.156
  118.7 4.2 %collective-permute-start.4 = (bf16[512,2,1,128]{3,0,2,1:T(8,128)(2,1)S(1)}, bf16[512,2,1,128]{3,0,2,1:T(8,128)(2,1)S(1)}, u32[]{:S(2)}, u32[]{:S(2)}) collective-permute-start(bf16[512,2,1,128]{3,0,2,1:T(8,128)(2,1)S(1)} %get-tuple-element.12), channel_id=1, source_target_pairs={{0,2},{2,4},{4,6},{1,3},{3,5},{5,7},{8,10},{10,12},{12,14},{9,11},... | collective-permute-start | bytes 786440 | tf_op jit(solution)/shard_map/ppermute | solution.py:15
  122.9 1.4 collective-permute-start.5
  124.3 1.7 fusion.76
  126.1 0.5 fusion.74
  126.6 0.5 fusion.78
  127.1 1.3 pad_maximum_fusion
  128.7 1.8 collective-permute-done.5
  130.5 1.0 constant_dynamic-update-slice_fusion.30
  131.5 2.3 %fusion.155 = (bf16[512,2,6,1]{3,0,2,1:T(8,128)(2,1)}, bf16[512,2,6,1]{3,0,2,1:T(8,128)(2,1)}) fusion(bf16[512,2,6,128]{3,0,2,1:T(8,128)(2,1)S(1)} %constant_dynamic-update-slice_fusion.30), kind=kLoop, calls=%fused_computation.231 | loop fusion | bytes 49152 | tf_op jit(solution)/shard_map/slice | solution.py:12
  133.8 1.7 copy.29
  135.5 1.3 collective-permute-start.6
  136.8 1.7 copy.30
  138.6 14.9 %collective-permute-start.7 = (bf16[512,2,6,1]{0,1,3,2:T(2,128)(2,1)S(1)}, bf16[512,2,6,1]{0,1,3,2:T(2,128)(2,1)S(1)}, u32[]{:S(2)}, u32[]{:S(2)}) collective-permute-start(bf16[512,2,6,1]{0,1,3,2:T(2,128)(2,1)S(1)} %copy.30), channel_id=1, source_target_pairs={{1,0},{3,2},{5,4},{7,6},{9,8},{11,10},{13,12},{15,14},{17,16},{19,... | collective-permute-start | bytes 36872 | tf_op jit(solution)/shard_map/ppermute | solution.py:17
  153.5 1.9 fusion.49
  155.4 1.7 convolution_bitcast_fusion.10
  157.1 1.0 copy.31
  158.1 1.6 copy.32
  159.7 3.7 %fusion.5 = bf16[512,4,6,130]{3,0,2,1:T(8,128)(2,1)S(1)} fusion(bf16[512,2,6,1]{3,0,2,1:T(8,128)(2,1)} %copy.32, bf16[512,2,6,128]{3,0,2,1:T(8,128)(2,1)S(1)} %constant_dynamic-update-slice_fusion.30, bf16[512,2,6,1]{3,0,2,1:T(8,128)(2,1)S(1)} %copy.31), kind=kLoop, calls=%fused_computation.7 | loop fusion | flops 19169280 | bytes 4792320 | tf_op jit(solution)/shard_map/concatenate | solution.py:13
  163.7 0.5 fusion.53
  164.2 0.5 fusion.55
  164.7 0.3 fusion.57
  165.0 0.5 fusion.59
  165.5 0.5 fusion.61
  166.1 0.3 fusion.63
  166.3 0.5 fusion.65
  167.0 0.8 fusion.68
  167.8 0.8 fusion.70
  168.6 0.6 fusion.72
  169.2 0.3 convolution_bitcast_fusion
  169.5 0.5 convolution_bitcast_fusion.1
  170.0 0.5 convolution_bitcast_fusion.2
  170.5 0.3 convolution_bitcast_fusion.3
  170.8 0.5 convolution_bitcast_fusion.4
  171.3 0.5 convolution_bitcast_fusion.5
  171.8 0.3 convolution_bitcast_fusion.6
  172.1 0.5 convolution_bitcast_fusion.7
  172.6 0.5 convolution_bitcast_fusion.8
  173.2 0.8 convolution_bitcast_fusion.11
  174.0 0.6 convolution_bitcast_fusion.9
  174.6 0.3 copy-done.10
  174.9 0.5 fusion.30
  175.4 0.7 copy-done.2
  176.4 0.7 fusion.31
  177.1 0.7 copy.41
  177.7 23.3 %all-reduce.6.cloned.1.call-done = f32[27,32,512]{2,1,0:T(8,128)} async-done(((f32[27,32,512]{2,1,0:T(8,128)}), f32[27,32,512]{2,1,0:T(8,128)}) %all-reduce.6.cloned.1.call-update) | async-done | bytes 1769488 | tf_op jit(solution)/shard_map/psum | solution.py:81
  201.0 3.0 %broadcast_multiply_fusion = f32[27,32,512]{2,1,0:T(8,128)} fusion(f32[27,32,512]{2,1,0:T(8,128)} %all-reduce.6.cloned.1.call-done), kind=kLoop, calls=%fused_computation.103 | loop fusion | flops 442368 | bytes 3538944 | tf_op jit(solution)/shard_map/mul | solution.py:81
  (60 shorter events, 3.0 us)
Async XLA Ops:
  7.2 14.2 %copy-start.11 = (u32[128]{0:T(128)S(1)}, u32[128]{0:T(128)}, u32[]{:S(2)}) copy-start(u32[128]{0:T(128)} %constant.11) | copy-start | bytes 1540
  7.2 20.4 %copy-start.8 = (bf16[32,2,4,128]{3,2,1,0:T(4,128)(2,1)S(1)}, bf16[32,2,4,128]{3,2,1,0:T(4,128)(2,1)}, u32[]{:S(2)}) copy-start(bf16[32,2,4,128]{3,2,1,0:T(4,128)(2,1)} %param.3) | copy-start | bytes 196612
  7.2 109.6 %all-gather.2.cloned.1.call-start = ((), (), s32[]{:S(2)}) async-start(), calls=%async_computation | async-start | bytes 1114112 | tf_op jit(solution)/shard_map/all_gather | solution.py:55
  8.1 7.2 %collective-permute-start = (bf16[32,2,1,128]{3,0,2,1:T(8,128)(2,1)S(1)}, bf16[32,2,1,128]{3,0,2,1:T(8,128)(2,1)S(1)}, u32[]{:S(2)}, u32[]{:S(2)}) collective-permute-start(bf16[32,2,1,128]{3,0,2,1:T(8,128)(2,1)S(1)} %get-tuple-element.35), channel_id=1, source_target_pairs={{0,2},{2,4},{4,6},{1,3},{3,5},{5,7},{8,10},{10,12},{12,14},{9,11},... | collective-permute-start | bytes 49160 | tf_op jit(solution)/shard_map/ppermute | solution.py:15
  14.0 187.0 %all-reduce.6.cloned.1.call-start = ((), (), s32[]{:S(2)}) async-start(), calls=%async_computation.1 | async-start | bytes 3538944 | tf_op jit(solution)/shard_map/psum | solution.py:81
  14.1 4.7 %collective-permute-start.1 = (bf16[32,2,1,128]{3,0,2,1:T(8,128)(2,1)S(1)}, bf16[32,2,1,128]{3,0,2,1:T(8,128)(2,1)S(1)}, u32[]{:S(2)}, u32[]{:S(2)}) collective-permute-start(bf16[32,2,1,128]{3,0,2,1:T(8,128)(2,1)S(1)} %get-tuple-element.34), channel_id=1, source_target_pairs={{2,0},{4,2},{6,4},{3,1},{5,3},{7,5},{10,8},{12,10},{14,12},{11,9},... | collective-permute-start | bytes 49160 | tf_op jit(solution)/shard_map/ppermute | solution.py:17
  18.8 7.6 %collective-permute-start.2 = (bf16[32,2,6,1]{3,0,2,1:T(8,128)(2,1)S(1)}, bf16[32,2,6,1]{3,0,2,1:T(8,128)(2,1)S(1)}, u32[]{:S(2)}, u32[]{:S(2)}) collective-permute-start(bf16[32,2,6,1]{3,0,2,1:T(8,128)(2,1)S(1)} %get-tuple-element.32), channel_id=1, source_target_pairs={{0,1},{2,3},{4,5},{6,7},{8,9},{10,11},{12,13},{14,15},{16,17},{18,... | collective-permute-start | bytes 2312 | tf_op jit(solution)/shard_map/ppermute | solution.py:15
  22.6 4.8 %collective-permute-start.3 = (bf16[32,2,6,1]{3,0,2,1:T(8,128)(2,1)S(1)}, bf16[32,2,6,1]{3,0,2,1:T(8,128)(2,1)S(1)}, u32[]{:S(2)}, u32[]{:S(2)}) collective-permute-start(bf16[32,2,6,1]{3,0,2,1:T(8,128)(2,1)S(1)} %get-tuple-element.33), channel_id=1, source_target_pairs={{1,0},{3,2},{5,4},{7,6},{9,8},{11,10},{13,12},{15,14},{17,16},{19,... | collective-permute-start | bytes 2312 | tf_op jit(solution)/shard_map/ppermute | solution.py:17
  28.7 2.0 copy-start.6
  28.9 1.9 copy-start.4
  116.8 9.3 %copy-start.5 = (bf16[288,2,4,128]{3,0,2,1:T(8,128)(2,1)S(1)}, bf16[288,2,4,128]{3,0,2,1:T(8,128)(2,1)}, u32[]{:S(2)}) copy-start(bf16[288,2,4,128]{3,0,2,1:T(8,128)(2,1)} %copy-done.4) | copy-start | bytes 1769476
  116.8 9.3 %copy-start.1 = (bf16[512,2,4,128]{3,0,2,1:T(8,128)(2,1)S(1)}, bf16[512,2,4,128]{3,0,2,1:T(8,128)(2,1)}, u32[]{:S(2)}) copy-start(bf16[512,2,4,128]{3,0,2,1:T(8,128)(2,1)} %all-gather.2.cloned.1.call-done) | copy-start | bytes 3145732
  118.7 9.8 %collective-permute-start.4 = (bf16[512,2,1,128]{3,0,2,1:T(8,128)(2,1)S(1)}, bf16[512,2,1,128]{3,0,2,1:T(8,128)(2,1)S(1)}, u32[]{:S(2)}, u32[]{:S(2)}) collective-permute-start(bf16[512,2,1,128]{3,0,2,1:T(8,128)(2,1)S(1)} %get-tuple-element.12), channel_id=1, source_target_pairs={{0,2},{2,4},{4,6},{1,3},{3,5},{5,7},{8,10},{10,12},{12,14},{9,11},... | collective-permute-start | bytes 786440 | tf_op jit(solution)/shard_map/ppermute | solution.py:15
  122.9 3.7 %copy-start.7 = (bf16[288,2,4,128]{3,0,2,1:T(8,128)(2,1)S(1)}, bf16[288,2,4,128]{3,0,2,1:T(8,128)(2,1)}, u32[]{:S(2)}) copy-start(bf16[288,2,4,128]{3,0,2,1:T(8,128)(2,1)} %copy-done.6) | copy-start | bytes 1769476
  122.9 7.6 %collective-permute-start.5 = (bf16[512,2,1,128]{3,0,2,1:T(8,128)(2,1)}, bf16[512,2,1,128]{3,0,2,1:T(8,128)(2,1)}, u32[]{:S(2)}, u32[]{:S(2)}) collective-permute-start(bf16[512,2,1,128]{3,0,2,1:T(8,128)(2,1)} %get-tuple-element.11), channel_id=1, source_target_pairs={{2,0},{4,2},{6,4},{3,1},{5,3},{7,5},{10,8},{12,10},{14,12},{11,9},... | collective-permute-start | bytes 786440 | tf_op jit(solution)/shard_map/ppermute | solution.py:17
  135.5 21.6 %collective-permute-start.6 = (bf16[512,2,6,1]{0,1,3,2:T(2,128)(2,1)S(1)}, bf16[512,2,6,1]{0,1,3,2:T(2,128)(2,1)S(1)}, u32[]{:S(2)}, u32[]{:S(2)}) collective-permute-start(bf16[512,2,6,1]{0,1,3,2:T(2,128)(2,1)S(1)} %copy.29), channel_id=1, source_target_pairs={{0,1},{2,3},{4,5},{6,7},{8,9},{10,11},{12,13},{14,15},{16,17},{18,... | collective-permute-start | bytes 36872 | tf_op jit(solution)/shard_map/ppermute | solution.py:15
  138.6 19.5 %collective-permute-start.7 = (bf16[512,2,6,1]{0,1,3,2:T(2,128)(2,1)S(1)}, bf16[512,2,6,1]{0,1,3,2:T(2,128)(2,1)S(1)}, u32[]{:S(2)}, u32[]{:S(2)}) collective-permute-start(bf16[512,2,6,1]{0,1,3,2:T(2,128)(2,1)S(1)} %copy.30), channel_id=1, source_target_pairs={{1,0},{3,2},{5,4},{7,6},{9,8},{11,10},{13,12},{15,14},{17,16},{19,... | collective-permute-start | bytes 36872 | tf_op jit(solution)/shard_map/ppermute | solution.py:17
  159.7 3.7 %copy-start.3 = (bf16[27,32,512]{2,1,0:T(8,128)(2,1)S(1)}, bf16[27,32,512]{2,1,0:T(8,128)(2,1)}, u32[]{:S(2)}) copy-start(bf16[27,32,512]{2,1,0:T(8,128)(2,1)} %param.4) | copy-start | bytes 2654212
  165.5 1.4 copy-start
  174.0 0.9 copy-start.10
  174.9 1.2 copy-start.2
  174.9 1.5 copy-start.9
Sparse Core Ops, SparseCore 0:
  14.1 47.5 all-gather.1
  128.6 72.3 all-reduce.5
where the time goes:
time: 213 us; the launch traced here: 211 us
  blocking collectives  82.8 us (39%)
  starting transfers between devices  32.7 us (15%)
  waiting for transfers between devices  28.4 us (13%)
  local copies, waits for them, and re-layouts  21.9 us (10%)
  matrix products  21.1 us (10%)
  between operations  15.1 us (7%)
  other arithmetic  8.86 us (4%)
    unnamed x1, blocking collectives  82.8 us
    psum x1, waiting for transfers between devices, shards(): kernel_grad = lax.psum(local_grad, ('sx', 'sy')) * scale  23.3 us
    ppermute x4, starting transfers between devices, with_halo(): lax.ppermute(head, axis, [((i + 1) % count, i) for i in range(ends)])  21.5 us
    dot_general x27, matrix products, shards(): jnp.einsum('io,ozxy->izxy', kernel[tap], window, preferred_element_type=j...  16.2 us
    ppermute x4, starting transfers between devices, with_halo(): lax.ppermute(tail, axis, [(i, (i + 1) % count) for i in range(ends)])  11.1 us
    unnamed x41, local copies, waits for them, and re-layouts  6.54 us
    ppermute x4, waiting for transfers between devices, with_halo(): lax.ppermute(head, axis, [((i + 1) % count, i) for i in range(ends)])  5.1 us
  transfers between devices with their start and end apart: 10, of which 4 were waited for; matrix products, arithmetic and copies ran while one was open for 21% of the time, Pallas kernels for 0%

commit v1 on v0

v1 whole, which is shorter than its diff:
```python
import functools

import jax
import jax.numpy as jnp
from jax import lax
from jax.experimental import pallas as pl
from jax.experimental.pallas import tpu as pltpu
from jax.sharding import PartitionSpec as P

MESH = pl.DeviceIdType.MESH
F32 = jnp.float32
BF16 = jnp.bfloat16


def nearby(i):
    return i + 1 - 2 * (i % 2), 3 - i, (i + 2) % 4


def body(
    scale, v_ref, c_ref, k_ref, resp_ref, vgrad_ref, kgrad_ref,
    rows32, full, other, edges, left, right, taps, kpart, kcore, kone, ktwo, kpiece,
    part, one, two, send_sem, recv_sem,
):
    c = lax.axis_index("ch")
    z = lax.axis_index("sx")
    p = lax.axis_index("sy")
    x, y = c // 4, c % 4
    x1, x3, x2 = nearby(x)
    y1, y3, y2 = nearby(y)
    z1, z3, z2 = nearby(z)
    up, down = (z + 1) % 4, (z + 3) % 4
    q = 1 - p

    def at(tx=None, ty=None, tz=None, tp=None):
        tx = x if tx is None else tx
        ty = y if ty is None else ty
        return {"ch": tx * 4 + ty, "sx": z if tz is None else tz, "sy": p if tp is None else tp}

    partners = [
        at(tx=x1), at(tx=x3), at(tx=x2), at(ty=y1), at(ty=y3), at(tz=z1), at(tz=z3),
        at(tp=q), at(tz=z1, tp=q), at(tz=z3, tp=q),
    ]
    barrier = pltpu.get_barrier_semaphore()
    for who in partners:
        pl.semaphore_signal(barrier, inc=1, device_id=who, device_id_type=MESH)

    for a, ref, g in ((0, v_ref, x), (1, c_ref, y)):
        rows32[a] = ref[...].astype(F32)
        for d in range(2):
            for b in range(4):
                block = rows32[a, pl.ds(d * 4 + b, 32, stride=8), :]
                full[a, d, g, :, 128 * (b + 1) : 128 * (b + 2)] = block.astype(BF16)
    pl.semaphore_wait(barrier, len(partners))

    count = [0]
    sends = []

    def push(src, dst, who):
        n = count[0]
        count[0] += 1
        copy = pltpu.make_async_remote_copy(
            src_ref=src, dst_ref=dst, send_sem=send_sem.at[n], recv_sem=recv_sem.at[n],
            device_id=who, device_id_type=MESH,
        )
        copy.start()
        sends.append(copy)
        return copy

    halo = []
    for a, g in ((0, x), (1, y)):
        low = full.at[a, :, g, :, pl.ds(128, 128)]
        high = full.at[a, :, g, :, pl.ds(512, 128)]
        halo.append(push(high, full.at[a, :, g, :, pl.ds(0, 128)], at(tz=up)))
        halo.append(push(low, full.at[a, :, g, :, pl.ds(640, 128)], at(tz=down)))
        halo.append(push(high, edges.at[a, 0], at(tz=up, tp=q)))
        halo.append(push(low, edges.at[a, 1], at(tz=down, tp=q)))
        halo.append(push(full.at[a, :, g, :, pl.ds(128, 512)], other.at[a], at(tp=q)))

    half = pl.ds(16 * p, 16)
    last = jnp.minimum(7 * z + 6, 26)
    tap_in = []
    for g in (x1, x3, x2):
        lanes = pl.ds(pl.multiple_of(128 * g, 128), 128)
        tap_in.append(push(k_ref.at[pl.ds(7 * z, 6), half, lanes], taps.at[pl.ds(7 * z, 6), x, half], at(tx=g)))
        tap_in.append(push(k_ref.at[last, half, lanes], taps.at[7 * z + 6, x, half], at(tx=g)))
    lanes = pl.ds(pl.multiple_of(128 * x, 128), 128)
    own = [
        pltpu.make_async_copy(k_ref.at[pl.ds(7 * z, 6), half, lanes], taps.at[pl.ds(7 * z, 6), x, half], send_sem.at[100]),
        pltpu.make_async_copy(k_ref.at[last, half, lanes], taps.at[7 * z + 6, x, half], send_sem.at[101]),
    ]
    for copy in own:
        copy.start()

    lane = lax.broadcasted_iota(jnp.int32, (64, 128), 1)
    has_low, has_high = z > 0, z < 3
    for a, g in ((0, x), (1, y)):
        for copy in halo[5 * a : 5 * a + 5]:
            copy.wait_recv()
        for b, ok in ((0, has_low), (5, has_high)):
            block = full[a, :, g, :, 128 * b : 128 * b + 128]
            full[a, :, g, :, 128 * b : 128 * b + 128] = jnp.where(ok, block, jnp.zeros_like(block))
        packed = jnp.zeros((64, 128), F32)
        for b in range(6):
            if b == 0:
                block = jnp.where(has_low, edges[a, 0].reshape(64, 128).astype(F32), 0.0)
            elif b == 5:
                block = jnp.where(has_high, edges[a, 1].reshape(64, 128).astype(F32), 0.0)
            else:
                block = other[a, :, :, 128 * b - 128 : 128 * b].reshape(64, 128).astype(F32)
            here = block if b == 0 else pltpu.roll(block, b, 1)
            there = pltpu.roll(block, b + 1, 1)
            packed = jnp.where(lane == b, jnp.where(p == 0, here, there), packed)
        full[a, :, g, :, 768:896] = packed.astype(BF16).reshape(2, 32, 128)

    def gather(ref, mine, one_way, other_way, to_one, to_other, cut):
        first = push(ref(mine, None), ref(mine, None), to_one)
        second = push(ref(mine, None), ref(mine, None), to_other)
        return first, second

    def whole(a, g):
        return full.at[a, :, g]

    def front(a, g):
        return full.at[a, :, g, :, pl.ds(0, 512)]

    def back(a, g):
        return full.at[a, :, g, :, pl.ds(512, 384)]

    rings = ((0, x, x1, x3, at(tx=x1), at(tx=x3)), (1, y, y1, y3, at(ty=y1), at(ty=y3)))
    near = []
    for a, g, g1, g3, to1, to3 in rings:
        near.append((push(whole(a, g), whole(a, g), to1), push(whole(a, g), whole(a, g), to3)))
    far = []
    for a, g, g1, g3, to1, to3 in rings:
        near[a][0].wait_recv()
        f = push(front(a, g1), front(a, g1), to3)
        near[a][1].wait_recv()
        far.append((f, push(back(a, g3), back(a, g3), to1)))

    for copy in own:
        copy.wait()
    for copy in tap_in:
        copy.wait_recv()

    def tap_piece(t, g0, n):
        return taps.at[pl.ds(7 * t, 7), pl.ds(g0, n), half]

    t1 = push(tap_piece(z, 0, 4), tap_piece(z, 0, 4), at(tz=z1))
    t3 = push(tap_piece(z, 0, 4), tap_piece(z, 0, 4), at(tz=z3))

    lane = lax.broadcasted_iota(jnp.int32, (256, 128), 1)
    for a in range(2):
        for copy in far[a]:
            copy.wait_recv()
        packed = full[a, :, :, :, 768:896].reshape(256, 128).astype(F32)
        for b in range(6):
            block = full[a, :, :, :, 128 * b : 128 * b + 128].reshape(256, 128).astype(F32)
            col = packed if b == 0 else pltpu.roll(packed, 128 - b, 1)
            shifted = jnp.where(lane == 0, jnp.where(p == 1, col, 0.0), pltpu.roll(block, 1, 1))
            left[a, :, 128 * b : 128 * b + 128] = shifted.astype(BF16)
            col = pltpu.roll(packed, 127 - b, 1)
            shifted = jnp.where(lane == 127, jnp.where(p == 0, col, 0.0), pltpu.roll(block, 127, 1))
            right[a, :, 128 * b : 128 * b + 128] = shifted.astype(BF16)

    t1.wait_recv()
    t1f = push(tap_piece(z1, 0, 2), tap_piece(z1, 0, 2), at(tz=z3))
    t3.wait_recv()
    t3f = push(tap_piece(z3, 2, 2), tap_piece(z3, 2, 2), at(tz=z1))

    def window(a, dy, dx):
        if dy == 1:
            return full[a, :, :, :, 128 * dx : 128 * dx + 512].reshape(256, 512)
        return (left if dy == 0 else right)[a, :, 128 * dx : 128 * dx + 512]

    cot = full[1, :, :, :, 128:640].reshape(256, 512)
    for dx in range(3):
        for dy in range(3):
            r = lax.dot_general(window(0, dy, dx), cot, (((1,), (1,)), ((), ())), preferred_element_type=F32)
            t = dx * 3 + dy
            kpart[t] = r[:128, 128:].reshape(4, 32, 128)
            kpart[9 + t] = (r[:128, :128] + r[128:, 128:]).reshape(4, 32, 128)
            kpart[18 + t] = r[128:, :128].reshape(4, 32, 128)
    kpart[27] = jnp.zeros((4, 32, 128), F32)
    their_half = pl.ds(pl.multiple_of(16 * q, 16), 16)
    core_sum = push(kpart.at[:, :, their_half], kcore, at(tp=q))

    t1f.wait_recv()
    t3f.wait_recv()
    tap_core = push(taps.at[:, :, half], taps.at[:, :, half], at(tp=q))

    my_half = pl.ds(pl.multiple_of(16 * p, 16), 16)
    core_sum.wait_recv()
    kcore[...] += kpart[:, :, my_half, :]

    def k_first(h, me, to, q1):
        rows = pl.ds(8 * h, 8)
        a0 = push(kcore.at[pl.ds(7 * q1, 7), :, rows], kone.at[h, 0], to)
        a1 = push(kcore.at[pl.ds(7 * z2, 7), :, rows], kone.at[h, 1], to)
        return a0, a1

    ka = k_first(0, z, at(tz=z3), z3)
    kb = k_first(1, z, at(tz=z1), z1)

    tap_core.wait_recv()

    def filt(dx, dy):
        t = dx * 3 + dy
        w0 = taps[t].reshape(128, 128)
        w1 = taps[9 + t].reshape(128, 128)
        w2 = taps[18 + t].reshape(128, 128)
        return jnp.concatenate([jnp.concatenate([w1, w0], 1), jnp.concatenate([w2, w1], 1)], 0)

    acc = jnp.zeros((256, 512), F32)
    for dx in range(3):
        for dy in range(3):
            acc += jnp.dot(filt(dx, dy), window(1, 2 - dy, 2 - dx), preferred_element_type=F32)
    part[1] = acc.reshape(2, 4, 32, 512)

    def first(a, h, to, g1, g2):
        cells = pl.ds(256 * h, 256)
        a0 = push(part.at[a, :, g1, :, cells], one.at[a, h, 0], to)
        a1 = push(part.at[a, :, g2, :, cells], one.at[a, h, 1], to)
        return a0, a1

    ba = first(1, 0, at(tx=x3), x3, x2)
    bb = first(1, 1, at(tx=x1), x1, x2)

    for copy in ka + kb:
        copy.wait_recv()
    kone[0, 1] += kcore[pl.ds(7 * z1, 7), :, 0:8, :]
    ka2 = push(kone.at[0, 1], ktwo.at[0], at(tz=z1))
    kone[1, 1] += kcore[pl.ds(7 * z3, 7), :, 8:16, :]
    kb2 = push(kone.at[1, 1], ktwo.at[1], at(tz=z3))

    acc = jnp.zeros((256, 512), F32)
    for dx in range(3):
        for dy in range(3):
            acc += lax.dot_general(
                filt(dx, dy), window(0, dy, dx), (((0,), (0,)), ((), ())), preferred_element_type=F32
            )
    part[0] = acc.reshape(2, 4, 32, 512)
    aa = first(0, 0, at(ty=y3), y3, y2)
    ab = first(0, 1, at(ty=y1), y1, y2)

    ka2.wait_recv()
    kb2.wait_recv()
    for h in range(2):
        kpiece[:, :, 8 * h : 8 * h + 8, :] = (
            kcore[pl.ds(7 * z, 7), :, 8 * h : 8 * h + 8, :] + kone[h, 0] + ktwo[h]
        ) * scale
    my_lanes = pl.ds(pl.multiple_of(128 * x, 128), 128)
    my_taps = pl.ds(7 * z, 7)
    there = kgrad_ref.at[my_taps, my_half, my_lanes]
    kx = [push(kpiece.at[:, g], there, at(tx=g)) for g in (x1, x3, x2)]
    kgrad_ref[my_taps, my_half, my_lanes] = kpiece[:, pl.ds(x, 1), :, :].reshape(7, 16, 128)

    def second(a, h, to, g, copies):
        for copy in copies:
            copy.wait_recv()
        one[a, h, 1] += part[a, :, g, :, 256 * h : 256 * h + 256]
        return push(one.at[a, h, 1], two.at[a, h], to)

    ba2 = second(1, 0, at(tx=x1), x1, ba)
    bb2 = second(1, 1, at(tx=x3), x3, bb)
    aa2 = second(0, 0, at(ty=y1), y1, aa)
    ab2 = second(0, 1, at(ty=y3), y3, ab)

    for copy in kx:
        copy.wait_recv()

    def k_piece(t, r, n):
        return kgrad_ref.at[pl.ds(7 * t, 7), pl.ds(pl.multiple_of(16 * p + r, 8), n), :]

    g1 = push(k_piece(z, 0, 16), k_piece(z, 0, 16), at(tz=z1))
    g3 = push(k_piece(z, 0, 16), k_piece(z, 0, 16), at(tz=z3))
    gc = [push(k_piece(z, 0, 16), k_piece(z, 0, 16), at(tp=q))]

    def finish(a, g, out_ref, copies):
        for h, copy in enumerate(copies):
            copy.wait_recv()
            for d in range(2):
                total = part[a, d, pl.ds(g, 1), :, 256 * h : 256 * h + 256].reshape(32, 256) + one[a, h, 0, d] + two[a, h, d]
                for b in range(2):
                    rows32[a, pl.ds(d * 4 + 2 * h + b, 32, stride=8), :] = total[:, 128 * b : 128 * b + 128]
        out_ref[...] = rows32[a].astype(BF16)

    finish(1, x, vgrad_ref, (ba2, bb2))
    finish(0, y, resp_ref, (aa2, ab2))

    g1.wait_recv()
    g1f = push(k_piece(z1, 0, 8), k_piece(z1, 0, 8), at(tz=z3))
    gc.append(push(k_piece(z1, 0, 16), k_piece(z1, 0, 16), at(tp=q)))
    g3.wait_recv()
    g3f = push(k_piece(z3, 8, 8), k_piece(z3, 8, 8), at(tz=z1))
    gc.append(push(k_piece(z3, 0, 16), k_piece(z3, 0, 16), at(tp=q)))
    g1f.wait_recv()
    g3f.wait_recv()
    gc.append(push(k_piece(z2, 0, 16), k_piece(z2, 0, 16), at(tp=q)))
    for copy in gc:
        copy.wait_recv()
    for copy in sends:
        copy.wait_send()


def shards(volume, kernel, cotangent):
    cells = 2 * 16 * 256
    scale = 1.0 / float(cells) ** 0.5
    vmem = pl.BlockSpec(memory_space=pltpu.VMEM)
    resp, vgrad, kgrad = pl.pallas_call(
        functools.partial(body, scale),
        out_shape=(
            jax.ShapeDtypeStruct((256, 128), BF16),
            jax.ShapeDtypeStruct((256, 128), BF16),
            jax.ShapeDtypeStruct((28, 32, 512), F32),
        ),
        in_specs=[vmem, vmem, pl.BlockSpec(memory_space=pl.ANY)],
        out_specs=(vmem, vmem, vmem),
        scratch_shapes=[
            pltpu.VMEM((2, 256, 128), F32),
            pltpu.VMEM((2, 2, 4, 32, 896), BF16),
            pltpu.VMEM((2, 2, 32, 512), BF16),
            pltpu.VMEM((2, 2, 2, 32, 128), BF16),
            pltpu.VMEM((2, 256, 768), BF16),
            pltpu.VMEM((2, 256, 768), BF16),
            pltpu.VMEM((28, 4, 32, 128), BF16),
            pltpu.VMEM((28, 4, 32, 128), F32),
            pltpu.VMEM((28, 4, 16, 128), F32),
            pltpu.VMEM((2, 2, 7, 4, 8, 128), F32),
            pltpu.VMEM((2, 7, 4, 8, 128), F32),
            pltpu.VMEM((7, 4, 16, 128), F32),
            pltpu.VMEM((2, 2, 4, 32, 512), F32),
            pltpu.VMEM((2, 2, 2, 2, 32, 256), F32),
            pltpu.VMEM((2, 2, 2, 32, 256), F32),
            pltpu.SemaphoreType.DMA((102,)),
            pltpu.SemaphoreType.DMA((102,)),
        ],
        compiler_params=pltpu.CompilerParams(
            collective_id=0, has_side_effects=True, vmem_limit_bytes=48 * 1024 * 1024
        ),
    )(volume.reshape(256, 128), cotangent.reshape(256, 128), kernel)
    return (resp.reshape(volume.shape), vgrad.reshape(volume.shape), kgrad[:27])


def solution(mesh):
    in_specs = (P("ch", None, "sx", "sy"), P(None, "ch", None), P("ch", None, "sx", "sy"))
    out_specs = (P("ch", None, "sx", "sy"), P("ch", None, "sx", "sy"), P(None, "ch", None))
    return jax.shard_map(shards, mesh=mesh, in_specs=in_specs, out_specs=out_specs, check_vma=False)
```

time: 213 us -> 61.8 us (0.29)
  blocking collectives: 82.8 us -> 0 us
  Pallas kernels: 0 us -> 55.4 us
  starting transfers between devices: 32.7 us -> 0 us
  waiting for transfers between devices: 28.4 us -> 0 us
  matrix products: 21.1 us -> 0 us
  local copies, waits for them, and re-layouts: 21.9 us -> 5.53 us
  between operations: 15.1 us -> 0.65 us
  other arithmetic: 8.86 us -> 0 us
    unnamed x1 -> x0, blocking collectives: 82.8 us -> none
    pallas_call x0 -> x1, Pallas kernels: none -> 55.4 us  [shards(): pl.pallas_call(functools.partial(body, scale), out_shape=(jax.ShapeDtypeS...]
    ppermute x8 -> x0, starting transfers between devices: 32.6 us -> none  [the longest x4 21.5 us: with_halo(): lax.ppermute(head, axis, [((i + 1) % count, i) for i in range(ends)])]
    psum x1 -> x0, waiting for transfers between devices: 23.3 us -> none  [shards(): kernel_grad = lax.psum(local_grad, ('sx', 'sy')) * scale]
    dot_general x33 -> x0, matrix products: 21.1 us -> none  [the longest x27 16.2 us: shards(): jnp.einsum('io,ozxy->izxy', kernel[tap], window, preferred_element_type=j...]
    slice x7 -> x1, local copies, waits for them, and re-layouts: 8.98 us -> 1.44 us  [shards(): return (resp.reshape(volume.shape), vgrad.reshape(volume.shape), kgrad[:27])]
    concatenate x4 -> x0, other arithmetic: 5.3 us -> none  [the longest x2 3.83 us: with_halo(): jnp.concatenate([lax.ppermute(tail, axis, [(i, (i + 1) % count) for i in...]
    ppermute x8 -> x0, waiting for transfers between devices: 5.11 us -> none  [the longest x4 5.1 us: with_halo(): lax.ppermute(head, axis, [((i + 1) % count, i) for i in range(ends)])]
  transfers between devices with their start and end apart: 10 -> 0, of which waited for: 4 -> 0; matrix products, arithmetic and copies ran while one was open for 21% -> 0% of each run, Pallas kernels for 0% -> 0%
where the time goes in v1:
time: 61.8 us; the launch traced here: 61.6 us
  Pallas kernels  55.4 us (90%)
  local copies, waits for them, and re-layouts  5.53 us (9%)
  between operations  0.65 us (1%)
    pallas_call x1, Pallas kernels, shards(): pl.pallas_call(functools.partial(body, scale), out_shape=(jax.ShapeDtypeS...  55.4 us
    unnamed x8, local copies, waits for them, and re-layouts  4.1 us
    slice x1, local copies, waits for them, and re-layouts, shards(): return (resp.reshape(volume.shape), vgrad.reshape(volume.shape), kgrad[:27])  1.44 us

profile of v1, /device:TPU:1, one launch (start us, length us, event | category | flops | bytes accessed | tf_op | source)
XLA Modules:
  0.0 61.6 jit_solution(3612026748015481622)
XLA Ops:
  0.6 0.0 copy-start
  0.6 1.2 %copy-done = bf16[27,32,512]{2,1,0:T(8,128)(2,1)S(1)} copy-done((bf16[27,32,512]{2,1,0:T(8,128)(2,1)S(1)}, bf16[27,32,512]{2,1,0:T(8,128)(2,1)}, u32[]{:S(2)}) %copy-start) | copy-done | bytes 884760
  1.8 0.0 copy-start.1
  1.8 0.8 %copy-done.1 = bf16[32,2,4,128]{3,2,1,0:T(4,128)(2,1)S(1)} copy-done((bf16[32,2,4,128]{3,2,1,0:T(4,128)(2,1)S(1)}, bf16[32,2,4,128]{3,2,1,0:T(4,128)(2,1)}, u32[]{:S(2)}) %copy-start.1) | copy-done | bytes 65560
  2.6 0.0 copy-start.2
  2.6 0.8 %copy-done.2 = bf16[32,2,4,128]{3,2,1,0:T(4,128)(2,1)S(1)} copy-done((bf16[32,2,4,128]{3,2,1,0:T(4,128)(2,1)S(1)}, bf16[32,2,4,128]{3,2,1,0:T(4,128)(2,1)}, u32[]{:S(2)}) %copy-start.2) | copy-done | bytes 65560
  3.5 55.4 %shard_map.58 = (bf16[256,128]{1,0:T(8,128)(2,1)S(1)}, bf16[256,128]{1,0:T(8,128)(2,1)S(1)}, f32[28,32,512]{2,1,0:T(8,128)S(1)}) custom-call(bf16[256,128]{1,0:T(8,128)(2,1)S(1)} %bitcast.4, bf16[256,128]{1,0:T(8,128)(2,1)S(1)} %bitcast.5, bf16[27,32,512]{2,1,0:T(8,128)(2,1)S(1)} %copy-done), custom_call_target="tpu_custom_call" | custom-call | tf_op jit(solution)/shard_map/pallas_call | solution.py:309
  58.9 1.4 %slice.3 = f32[27,32,512]{2,1,0:T(8,128)} slice(f32[28,32,512]{2,1,0:T(8,128)S(1)} %get-tuple-element.8), slice={[0:27], [0:32], [0:512]} | slice | bytes 3538944 | tf_op jit(solution)/shard_map/slice | solution.py:341
  60.3 0.6 %copy.8 = bf16[32,2,4,128]{3,2,1,0:T(4,128)(2,1)} copy(bf16[32,2,4,128]{3,2,1,0:T(4,128)(2,1)S(1)} %bitcast.7) | data formatting | bytes 131072
  61.0 0.6 %copy.9 = bf16[32,2,4,128]{3,2,1,0:T(4,128)(2,1)} copy(bf16[32,2,4,128]{3,2,1,0:T(4,128)(2,1)S(1)} %bitcast.6) | data formatting | bytes 131072
Async XLA Ops:
  0.6 1.2 %copy-start = (bf16[27,32,512]{2,1,0:T(8,128)(2,1)S(1)}, bf16[27,32,512]{2,1,0:T(8,128)(2,1)}, u32[]{:S(2)}) copy-start(bf16[27,32,512]{2,1,0:T(8,128)(2,1)} %k_ref.1) | copy-start | bytes 2654212
  1.8 0.8 %copy-start.1 = (bf16[32,2,4,128]{3,2,1,0:T(4,128)(2,1)S(1)}, bf16[32,2,4,128]{3,2,1,0:T(4,128)(2,1)}, u32[]{:S(2)}) copy-start(bf16[32,2,4,128]{3,2,1,0:T(4,128)(2,1)} %param.3) | copy-start | bytes 196612
  2.6 0.8 %copy-start.2 = (bf16[32,2,4,128]{3,2,1,0:T(4,128)(2,1)S(1)}, bf16[32,2,4,128]{3,2,1,0:T(4,128)(2,1)}, u32[]{:S(2)}) copy-start(bf16[32,2,4,128]{3,2,1,0:T(4,128)(2,1)} %param.5) | copy-start | bytes 196612

commit v2 on v1

v2 whole, which is shorter than its diff:
```python
import functools

import jax
import jax.numpy as jnp
from jax import lax
from jax.experimental import pallas as pl
from jax.experimental.pallas import tpu as pltpu
from jax.sharding import PartitionSpec as P

MESH = pl.DeviceIdType.MESH
F32 = jnp.float32
BF16 = jnp.bfloat16
SPAN = 86.0
ORDER = [(dz, dx, dy) for dy in (1, 0, 2) for dz in range(3) for dx in range(3)]


def nearby(i):
    return i + 1 - 2 * (i % 2), 3 - i, (i + 2) % 4


def encode(values):
    top = jnp.max(jnp.abs(values), axis=0)
    unit = (jnp.maximum(top, 1e-30) * 1.01).astype(BF16)
    gain = SPAN / unit.astype(F32)
    return jnp.exp(values * gain[None]).astype(BF16), unit


def decode(code, unit):
    return jnp.log(code.astype(F32)) * (unit.astype(F32) * (1.0 / SPAN))[None]


def body(
    scale, v_ref, c_ref, k_ref, resp_ref, vgrad_ref, kcode_ref,
    bricks, rows32, full, other, left, right, taps, kpart, kcore, rsend, rland, fin,
    part, one, two, send_sem, recv_sem, load_sem,
):
    c = lax.axis_index("ch")
    z = lax.axis_index("sx")
    p = lax.axis_index("sy")
    x, y = c // 4, c % 4
    x1, x3, x2 = nearby(x)
    y1, y3, y2 = nearby(y)
    z1, z3, z2 = nearby(z)
    up, down = (z + 1) % 4, (z + 3) % 4
    q = 1 - p

    def at(tx=None, ty=None, tz=None, tp=None):
        tx = x if tx is None else tx
        ty = y if ty is None else ty
        return {"ch": tx * 4 + ty, "sx": z if tz is None else tz, "sy": p if tp is None else tp}

    partners = [at(tx=a, tz=b) for a in (x2, x1, x3, x) for b in (z2, z1, z3, z)][:-1]
    partners += [at(ty=y2), at(ty=y1), at(ty=y3), at(tp=q)]
    barrier = pltpu.get_barrier_semaphore()
    for who in partners:
        pl.semaphore_signal(barrier, inc=1, device_id=who, device_id_type=MESH)

    half = pl.ds(pl.multiple_of(16 * p, 16), 16)
    their_half = pl.ds(pl.multiple_of(16 * q, 16), 16)
    last = jnp.minimum(7 * z + 6, 26)
    lanes = pl.ds(pl.multiple_of(128 * x, 128), 128)
    loads = [
        pltpu.make_async_copy(v_ref, bricks.at[0], load_sem.at[0]),
        pltpu.make_async_copy(c_ref, bricks.at[1], load_sem.at[1]),
        pltpu.make_async_copy(k_ref.at[pl.ds(7 * z, 6), half, lanes], taps.at[pl.ds(7 * z, 6), x, half], load_sem.at[2]),
        pltpu.make_async_copy(k_ref.at[last, half, lanes], taps.at[7 * z + 6, x, half], load_sem.at[3]),
    ]
    for copy in loads:
        copy.start()

    for a, g in ((0, x), (1, y)):
        loads[a].wait()
        rows32[a] = bricks[a].astype(F32)
        for d in range(2):
            for b in range(4):
                block = rows32[a, pl.ds(d * 4 + b, 32, stride=8), :]
                full[a, d, g, :, 128 * (b + 1) : 128 * (b + 2)] = block.astype(BF16)
    pl.semaphore_wait(barrier, len(partners))

    count = [0]
    sends = []

    def push(src, dst, who):
        n = count[0]
        count[0] += 1
        copy = pltpu.make_async_remote_copy(
            src_ref=src, dst_ref=dst, send_sem=send_sem.at[n], recv_sem=recv_sem.at[n],
            device_id=who, device_id_type=MESH,
        )
        copy.start()
        sends.append(copy)
        return copy

    def sent(copy):
        copy.wait_send()
        sends[:] = [s for s in sends if s is not copy]

    def cells(a, g, first, n):
        return full.at[a, :, g, :, pl.ds(128 * first, 128 * n)]

    vol_in = {}
    for k, g in (("2", x2), ("1", x1), ("3", x3), ("0", x)):
        vol_in[k] = [
            push(cells(0, x, 4, 1), cells(0, x, 0, 1), at(tx=g, tz=up)),
            push(cells(0, x, 1, 1), cells(0, x, 5, 1), at(tx=g, tz=down)),
        ]
        if k != "0":
            vol_in[k].append(push(cells(0, x, 1, 4), cells(0, x, 1, 4), at(tx=g)))
    cot_in = [push(cells(1, y, 1, 4), cells(1, y, 1, 4), at(ty=g)) for g in (y2, y1, y3)]

    tap_in = []
    for g in (x2, x1, x3):
        away = pl.ds(pl.multiple_of(128 * g, 128), 128)
        tap_in.append(push(k_ref.at[pl.ds(7 * z, 6), half, away], taps.at[pl.ds(7 * z, 6), x, half], at(tx=g)))
        tap_in.append(push(k_ref.at[last, half, away], taps.at[7 * z + 6, x, half], at(tx=g)))

    cross_v = []
    for k, g in (("0", x), ("1", x1), ("3", x3), ("2", x2)):
        for copy in vol_in[k]:
            copy.wait_recv()
        cross_v.append(push(full.at[0, :, g], other.at[0, :, g], at(tp=q)))
    for copy in cot_in:
        copy.wait_recv()
    every = pl.ds(0, 4)
    cot_edges = [
        push(full.at[1, :, every, :, pl.ds(512, 128)], full.at[1, :, every, :, pl.ds(0, 128)], at(tz=up)),
        push(full.at[1, :, every, :, pl.ds(128, 128)], full.at[1, :, every, :, pl.ds(640, 128)], at(tz=down)),
    ]

    def clear(ref, a):
        @pl.when(z == 0)
        def _():
            ref[a, :, :, :, 0:128] = jnp.zeros((2, 4, 32, 128), BF16)

        @pl.when(z == 3)
        def _():
            ref[a, :, :, :, 640:768] = jnp.zeros((2, 4, 32, 128), BF16)

    for copy in cross_v:
        sent(copy)
    clear(full, 0)

    def window(a, dy, dx):
        if dy == 1:
            return full[a, :, :, :, 128 * dx : 128 * dx + 512].reshape(256, 512)
        return (left if dy == 0 else right)[a, :, 128 * dx : 128 * dx + 512]

    lane = lax.broadcasted_iota(jnp.int32, (256, 128), 1)

    def shift(a):
        for b in range(6):
            mine = full[a, :, :, :, 128 * b : 128 * b + 128].reshape(256, 128).astype(F32)
            theirs = other[a, :, :, :, 128 * b : 128 * b + 128].reshape(256, 128).astype(F32)
            before = jnp.where(lane == 127, jnp.where(p == 1, theirs, 0.0), mine)
            after = jnp.where(lane == 0, jnp.where(p == 0, theirs, 0.0), mine)
            left[a, :, 128 * b : 128 * b + 128] = pltpu.roll(before, 1, 1).astype(BF16)
            right[a, :, 128 * b : 128 * b + 128] = pltpu.roll(after, 127, 1).astype(BF16)

    cot = full[1, :, :, :, 128:640].reshape(256, 512)
    core_in = []
    kpart[27] = jnp.zeros((4, 32, 128), F32)
    for s, dy in enumerate((1, 0, 2)):
        if s == 1:
            for copy in cross_v:
                copy.wait_recv()
            clear(other, 0)
            shift(0)
        for dx in range(3):
            r = lax.dot_general(window(0, dy, dx), cot, (((1,), (1,)), ((), ())), preferred_element_type=F32)
            kpart[9 * s + dx] = r[:128, 128:].reshape(4, 32, 128)
            kpart[9 * s + 3 + dx] = (r[:128, :128] + r[128:, 128:]).reshape(4, 32, 128)
            kpart[9 * s + 6 + dx] = r[128:, :128].reshape(4, 32, 128)
        span = pl.ds(9 * s, 9 if s < 2 else 10)
        core_in.append(push(kpart.at[span, :, their_half], kcore.at[span], at(tp=q)))

    for copy in loads[2:]:
        copy.wait()
    for copy in tap_in:
        copy.wait_recv()

    def tap_piece(t, g0, n):
        return taps.at[pl.ds(7 * t, 7), pl.ds(g0, n), half]

    t1 = push(tap_piece(z, 0, 4), tap_piece(z, 0, 4), at(tz=z1))
    t3 = push(tap_piece(z, 0, 4), tap_piece(z, 0, 4), at(tz=z3))

    for copy in core_in:
        copy.wait_recv()
    z_in = []
    for n, g in enumerate((z2, z1, z3)):
        span = pl.ds(7 * g, 7)
        total = (kcore[span] + kpart[span, :, half, :]).reshape(28, 16, 128)
        code, unit = encode(total)
        rsend[n, 0:28] = code
        rsend[n, 28] = unit
        z_in.append(push(rsend.at[n], rland.at[n], at(tz=g)))

    for copy in cot_edges:
        copy.wait_recv()
    cross_c = push(full.at[1], other.at[1], at(tp=q))
    t1.wait_recv()
    t1f = push(tap_piece(z1, 0, 2), tap_piece(z1, 0, 2), at(tz=z3))
    t3.wait_recv()
    t3f = push(tap_piece(z3, 2, 2), tap_piece(z3, 2, 2), at(tz=z1))
    cross_c.wait_recv()
    for copy in [cross_c] + cot_edges:
        sent(copy)
    clear(full, 1)
    clear(other, 1)
    shift(1)
    t1f.wait_recv()
    t3f.wait_recv()
    tap_core = push(taps.at[:, :, half], taps.at[:, :, half], at(tp=q))
    tap_core.wait_recv()

    def filt(dx, dy):
        t = dx * 3 + dy
        w0 = taps[t].reshape(128, 128)
        w1 = taps[9 + t].reshape(128, 128)
        w2 = taps[18 + t].reshape(128, 128)
        return jnp.concatenate([jnp.concatenate([w1, w0], 1), jnp.concatenate([w2, w1], 1)], 0)

    def first(a, h, to, g1, g2):
        cut = pl.ds(256 * h, 256)
        a0 = push(part.at[a, :, g1, :, cut], one.at[a, h, 0], to)
        a1 = push(part.at[a, :, g2, :, cut], one.at[a, h, 1], to)
        return a0, a1

    acc = jnp.zeros((256, 512), F32)
    for dx in range(3):
        for dy in range(3):
            acc += jnp.dot(filt(dx, dy), window(1, 2 - dy, 2 - dx), preferred_element_type=F32)
    part[1] = acc.reshape(2, 4, 32, 512)
    ba = first(1, 0, at(tx=x3), x3, x2)
    bb = first(1, 1, at(tx=x1), x1, x2)

    for copy in z_in:
        copy.wait_recv()
    mine = pl.ds(7 * z, 7)
    total = (kcore[mine] + kpart[mine, :, half, :]).reshape(28, 16, 128)
    for n in range(3):
        total = total + decode(rland[n, 0:28], rland[n, 28])
    total = (total * scale).reshape(7, 4, 16, 128)
    for g in range(4):
        code, unit = encode(total[:, g])
        fin[g, 0:7] = code
        fin[g, 7] = unit
    spread = {}
    for kz, gz in (("2", z2), ("1", z1), ("3", z3), ("0", z)):
        for kx, gx in (("2", x2), ("1", x1), ("3", x3), ("0", x)):
            if kz + kx != "00":
                there = kcode_ref.at[z, x, :, half, :]
                spread[kz + kx] = push(fin.at[gx], there, at(tx=gx, tz=gz))
    stores = [pltpu.make_async_copy(fin.at[x], kcode_ref.at[z, x, :, half, :], load_sem.at[4])]
    stores[0].start()

    acc = jnp.zeros((256, 512), F32)
    for dx in range(3):
        for dy in range(3):
            acc += lax.dot_general(
                filt(dx, dy), window(0, dy, dx), (((0,), (0,)), ((), ())), preferred_element_type=F32
            )
    part[0] = acc.reshape(2, 4, 32, 512)
    aa = first(0, 0, at(ty=y3), y3, y2)
    ab = first(0, 1, at(ty=y1), y1, y2)

    def second(a, h, to, g, copies):
        for copy in copies:
            copy.wait_recv()
        one[a, h, 1] += part[a, :, g, :, 256 * h : 256 * h + 256]
        return push(one.at[a, h, 1], two.at[a, h], to)

    def finish(a, g, out_ref, copies):
        for h, copy in enumerate(copies):
            copy.wait_recv()
            for d in range(2):
                total = part[a, d, pl.ds(g, 1), :, 256 * h : 256 * h + 256].reshape(32, 256) + one[a, h, 0, d] + two[a, h, d]
                for b in range(2):
                    rows32[a, pl.ds(d * 4 + 2 * h + b, 32, stride=8), :] = total[:, 128 * b : 128 * b + 128]
        bricks[a] = rows32[a].astype(BF16)
        stores.append(pltpu.make_async_copy(bricks.at[a], out_ref, load_sem.at[5 + a]))
        stores[-1].start()

    ba2 = second(1, 0, at(tx=x1), x1, ba)
    bb2 = second(1, 1, at(tx=x3), x3, bb)
    aa2 = second(0, 0, at(ty=y1), y1, aa)
    ab2 = second(0, 1, at(ty=y3), y3, ab)

    stores[0].wait()

    def hand_on(kz, gz):
        for kx in "0132":
            if kz + kx != "00":
                spread[kz + kx].wait_recv()
        return push(kcode_ref.at[gz, :, :, half, :], kcode_ref.at[gz, :, :, half, :], at(tp=q))

    k_in = [hand_on("0", z), hand_on("1", z1), hand_on("3", z3)]
    finish(1, x, vgrad_ref, (ba2, bb2))
    finish(0, y, resp_ref, (aa2, ab2))
    k_in.append(hand_on("2", z2))
    for copy in k_in:
        copy.wait_recv()
    for copy in stores[1:]:
        copy.wait()
    for copy in sends:
        copy.wait_send()


def write(resp_ref, vgrad_ref, kcode_ref, resp_out, vgrad_out, kgrad_out, cells, codes, wide, sem):
    loads = [pltpu.make_async_copy(kcode_ref.at[g], codes.at[g], sem.at[29 + g]) for g in range(4)]
    for copy in loads:
        copy.start()
    small = [
        pltpu.make_async_copy(resp_ref, cells.at[0], sem.at[33]),
        pltpu.make_async_copy(vgrad_ref, cells.at[1], sem.at[34]),
    ]
    for copy in small:
        copy.start()
    copies = [
        pltpu.make_async_copy(cells.at[0], resp_out, sem.at[27]),
        pltpu.make_async_copy(cells.at[1], vgrad_out, sem.at[28]),
    ]
    for load, copy in zip(small, copies):
        load.wait()
        copy.start()
    for n, (dz, dx, dy) in enumerate(ORDER):
        t = dz * 9 + dx * 3 + dy
        if n % 7 == 0:
            loads[n // 7].wait()
        for g in range(4):
            code = codes[n // 7, g, n % 7].astype(F32)
            unit = codes[n // 7, g, 7].astype(F32) * (1.0 / SPAN)
            wide[t, :, 128 * g : 128 * g + 128] = jnp.log(code) * unit
        copy = pltpu.make_async_copy(wide.at[t], kgrad_out.at[t], sem.at[n])
        copy.start()
        copies.append(copy)
    for copy in copies:
        copy.wait()


def shards(volume, kernel, cotangent):
    cells = 2 * 16 * 256
    scale = 1.0 / float(cells) ** 0.5
    hbm = pl.BlockSpec(memory_space=pl.ANY)
    resp, vgrad, kcode = pl.pallas_call(
        functools.partial(body, scale),
        out_shape=(
            jax.ShapeDtypeStruct((256, 128), BF16),
            jax.ShapeDtypeStruct((256, 128), BF16),
            jax.ShapeDtypeStruct((4, 4, 8, 32, 128), BF16),
        ),
        in_specs=[hbm, hbm, hbm],
        out_specs=(hbm, hbm, hbm),
        scratch_shapes=[
            pltpu.VMEM((2, 256, 128), BF16),
            pltpu.VMEM((2, 256, 128), F32),
            pltpu.VMEM((2, 2, 4, 32, 768), BF16),
            pltpu.VMEM((2, 2, 4, 32, 768), BF16),
            pltpu.VMEM((2, 256, 768), BF16),
            pltpu.VMEM((2, 256, 768), BF16),
            pltpu.VMEM((28, 4, 32, 128), BF16),
            pltpu.VMEM((28, 4, 32, 128), F32),
            pltpu.VMEM((28, 4, 16, 128), F32),
            pltpu.VMEM((3, 29, 16, 128), BF16),
            pltpu.VMEM((3, 29, 16, 128), BF16),
            pltpu.VMEM((4, 8, 16, 128), BF16),
            pltpu.VMEM((2, 2, 4, 32, 512), F32),
            pltpu.VMEM((2, 2, 2, 2, 32, 256), F32),
            pltpu.VMEM((2, 2, 2, 32, 256), F32),
            pltpu.SemaphoreType.DMA((80,)),
            pltpu.SemaphoreType.DMA((80,)),
            pltpu.SemaphoreType.DMA((7,)),
        ],
        compiler_params=pltpu.CompilerParams(
            collective_id=0, has_side_effects=True, vmem_limit_bytes=56 * 1024 * 1024
        ),
    )(volume.reshape(256, 128), cotangent.reshape(256, 128), kernel)
    resp, vgrad, kgrad = pl.pallas_call(
        write,
        out_shape=(
            jax.ShapeDtypeStruct((256, 128), BF16),
            jax.ShapeDtypeStruct((256, 128), BF16),
            jax.ShapeDtypeStruct((27, 32, 512), F32),
        ),
        in_specs=[hbm, hbm, hbm],
        out_specs=(hbm, hbm, hbm),
        scratch_shapes=[
            pltpu.VMEM((2, 256, 128), BF16),
            pltpu.VMEM((4, 4, 8, 32, 128), BF16),
            pltpu.VMEM((27, 32, 512), F32),
            pltpu.SemaphoreType.DMA((35,)),
        ],
        compiler_params=pltpu.CompilerParams(vmem_limit_bytes=56 * 1024 * 1024),
    )(resp, vgrad, kcode)
    return (resp.reshape(volume.shape), vgrad.reshape(volume.shape), kgrad)


def solution(mesh):
    in_specs = (P("ch", None, "sx", "sy"), P(None, "ch", None), P("ch", None, "sx", "sy"))
    out_specs = (P("ch", None, "sx", "sy"), P("ch", None, "sx", "sy"), P(None, "ch", None))
    return jax.shard_map(shards, mesh=mesh, in_specs=in_specs, out_specs=out_specs, check_vma=False)
```

time: 61.8 us -> 49.6 us (0.80)
  Pallas kernels: 55.4 us -> 48.8 us
  local copies, waits for them, and re-layouts: 5.53 us -> 0 us
    pallas_call x1, Pallas kernels: 55.4 us -> 46.1 us  [shards(): pl.pallas_call(functools.partial(body, scale), out_shape=(jax.ShapeDtypeS...]
    unnamed x8 -> x0, local copies, waits for them, and re-layouts: 4.1 us -> none
    pallas_call x0 -> x1, Pallas kernels: none -> 2.69 us  [shards(): pl.pallas_call(write, out_shape=(jax.ShapeDtypeStruct((256, 128), BF16),...]
    slice x1 -> x0, local copies, waits for them, and re-layouts: 1.44 us -> none  [shards(): return (resp.reshape(volume.shape), vgrad.reshape(volume.shape), kgrad[:27])]
where the time goes in v2:
time: 49.6 us; the launch traced here: 49.4 us
  Pallas kernels  48.8 us (98%)
  between operations  0.64 us (1%)
    pallas_call x1, Pallas kernels, shards(): pl.pallas_call(functools.partial(body, scale), out_shape=(jax.ShapeDtypeS...  46.1 us
    pallas_call x1, Pallas kernels, shards(): pl.pallas_call(write, out_shape=(jax.ShapeDtypeStruct((256, 128), BF16),...  2.69 us

profile of v2, /device:TPU:1, one launch (start us, length us, event | category | flops | bytes accessed | tf_op | source)
XLA Modules:
  0.0 49.4 jit_solution(7367156231018507285)
XLA Ops:
  0.6 46.1 %shard_map.58 = (bf16[256,128]{1,0:T(8,128)(2,1)}, bf16[256,128]{1,0:T(8,128)(2,1)}, bf16[4,4,8,32,128]{4,3,2,1,0:T(8,128)(2,1)}) custom-call(bf16[256,128]{1,0:T(8,128)(2,1)} %bitcast.4, bf16[256,128]{1,0:T(8,128)(2,1)} %bitcast.5, bf16[27,32,512]{2,1,0:T(8,128)(2,1)} %k_ref.1), custom_call_target="tpu_custom_call" | custom-call | tf_op jit(solution)/shard_map/pallas_call | solution.py:345
  46.7 2.7 %shard_map.59 = (bf16[256,128]{1,0:T(8,128)(2,1)}, bf16[256,128]{1,0:T(8,128)(2,1)}, f32[27,32,512]{2,1,0:T(8,128)}) custom-call(bf16[256,128]{1,0:T(8,128)(2,1)} %get-tuple-element.9.resp_ref, bf16[256,128]{1,0:T(8,128)(2,1)} %get-tuple-element.10.vgrad_ref, bf16[4,4,8,32,128]{4,3,2,1,0:T(8,128)(2,1)} %get-tuple-element.11.kcode_ref), custom_call_target="tpu_custom_call" | custom-call | tf_op jit(solution)/shard_map/pallas_call | solution.py:378

commit v3 on v2

v3 whole, which is shorter than its diff:
```python
import functools

import jax
import jax.numpy as jnp
from jax import lax
from jax.experimental import pallas as pl
from jax.experimental.pallas import tpu as pltpu
from jax.sharding import PartitionSpec as P

MESH = pl.DeviceIdType.MESH
F32 = jnp.float32
BF16 = jnp.bfloat16
SPAN = 86.0
ORDER = [(dz, dx, dy) for dy in (1, 0, 2) for dz in range(3) for dx in range(3)]


def nearby(i):
    return i + 1 - 2 * (i % 2), 3 - i, (i + 2) % 4


def encode(values):
    top = jnp.max(jnp.abs(values), axis=0)
    unit = (jnp.maximum(top, 1e-30) * 1.01).astype(BF16)
    gain = SPAN / unit.astype(F32)
    return jnp.exp(values * gain[None]).astype(BF16), unit


def decode(code, unit):
    return jnp.log(code.astype(F32)) * (unit.astype(F32) * (1.0 / SPAN))[None]


class Move:
    def __init__(self, copy, may_send, may_recv):
        self.copy, self.may_send, self.may_recv = copy, may_send, may_recv
        self.when(may_send, copy.start)

    @staticmethod
    def when(may, act):
        if may is None:
            act()
        else:
            pl.when(may)(lambda: act())

    def wait_send(self):
        self.when(self.may_send, self.copy.wait_send)

    def wait_recv(self):
        self.when(self.may_recv, self.copy.wait_recv)


def body(
    scale, v_ref, c_ref, k_ref, resp_ref, vgrad_ref, kcode_ref,
    bricks, rows32, full, other, left, right, taps, kpart, kcore, rsend, rland, fin,
    part, one, two, send_sem, recv_sem, load_sem,
):
    c = lax.axis_index("ch")
    z = lax.axis_index("sx")
    p = lax.axis_index("sy")
    x, y = c // 4, c % 4
    x1, x3, x2 = nearby(x)
    y1, y3, y2 = nearby(y)
    z1, z3, z2 = nearby(z)
    up, down = (z + 1) % 4, (z + 3) % 4
    q = 1 - p

    def at(tx=None, ty=None, tz=None, tp=None):
        tx = x if tx is None else tx
        ty = y if ty is None else ty
        return {"ch": tx * 4 + ty, "sx": z if tz is None else tz, "sy": p if tp is None else tp}

    partners = [at(tx=a, tz=b) for a in (x2, x1, x3, x) for b in (z2, z1, z3, z)][:-1]
    partners += [at(ty=y2), at(ty=y1), at(ty=y3), at(tp=q)]
    barrier = pltpu.get_barrier_semaphore()
    for who in partners:
        pl.semaphore_signal(barrier, inc=1, device_id=who, device_id_type=MESH)

    half = pl.ds(pl.multiple_of(16 * p, 16), 16)
    their_half = pl.ds(pl.multiple_of(16 * q, 16), 16)
    loads = [
        pltpu.make_async_copy(v_ref, bricks.at[0], load_sem.at[0]),
        pltpu.make_async_copy(c_ref, bricks.at[1], load_sem.at[1]),
        pltpu.make_async_copy(
            k_ref.at[:, :, pl.ds(pl.multiple_of(128 * x, 128), 128)], taps.at[:, x], load_sem.at[2]
        ),
    ]
    for copy in loads:
        copy.start()

    @pl.when(z == 0)
    def _():
        full[:, :, :, :, 0:128] = jnp.zeros((2, 2, 4, 32, 128), BF16)

    @pl.when(z == 3)
    def _():
        full[:, :, :, :, 640:768] = jnp.zeros((2, 2, 4, 32, 128), BF16)

    kpart[27] = jnp.zeros((4, 32, 128), F32)

    for a, g in ((0, x), (1, y)):
        loads[a].wait()
        rows32[a] = bricks[a].astype(F32)
        for d in range(2):
            for b in range(4):
                block = rows32[a, pl.ds(d * 4 + b, 32, stride=8), :]
                full[a, d, g, :, 128 * (b + 1) : 128 * (b + 2)] = block.astype(BF16)
    pl.semaphore_wait(barrier, len(partners))

    count = [0]
    sends = []

    def push(src, dst, who, may_send=None, may_recv=None):
        n = count[0]
        count[0] += 1
        copy = pltpu.make_async_remote_copy(
            src_ref=src, dst_ref=dst, send_sem=send_sem.at[n], recv_sem=recv_sem.at[n],
            device_id=who, device_id_type=MESH,
        )
        move = Move(copy, may_send, may_recv)
        sends.append(move)
        return move

    def cells(a, g, first, n):
        return full.at[a, :, g, :, pl.ds(128 * first, 128 * n)]

    vol_in = {}
    for k, g in (("2", x2), ("1", x1), ("3", x3), ("0", x)):
        vol_in[k] = [
            push(cells(0, x, 4, 1), cells(0, x, 0, 1), at(tx=g, tz=up), z < 3, z > 0),
            push(cells(0, x, 1, 1), cells(0, x, 5, 1), at(tx=g, tz=down), z > 0, z < 3),
        ]
        if k != "0":
            vol_in[k].append(push(cells(0, x, 1, 4), cells(0, x, 1, 4), at(tx=g)))
    cot_in = [push(cells(1, y, 1, 4), cells(1, y, 1, 4), at(ty=g)) for g in (y2, y1, y3)]

    def send_taps():
        return [
            push(k_ref.at[:, half, pl.ds(pl.multiple_of(128 * g, 128), 128)], taps.at[:, x, half], at(tx=g))
            for g in (x2, x1, x3)
        ]

    tap_in = send_taps()

    cross_v = []
    for k, g in (("0", x), ("1", x1), ("3", x3), ("2", x2)):
        for copy in vol_in[k]:
            copy.wait_recv()
        cross_v.append(push(full.at[0, :, g], other.at[0, :, g], at(tp=q)))
    for copy in cot_in:
        copy.wait_recv()
    every = pl.ds(0, 4)
    cot_edges = [
        push(
            full.at[1, :, every, :, pl.ds(512, 128)], full.at[1, :, every, :, pl.ds(0, 128)], at(tz=up), z < 3, z > 0
        ),
        push(
            full.at[1, :, every, :, pl.ds(128, 128)], full.at[1, :, every, :, pl.ds(640, 128)], at(tz=down), z > 0, z < 3
        ),
    ]

    def window(a, dy, dx):
        if dy == 1:
            return full[a, :, :, :, 128 * dx : 128 * dx + 512].reshape(256, 512)
        return (left if dy == 0 else right)[a, :, 128 * dx : 128 * dx + 512]

    lane = lax.broadcasted_iota(jnp.int32, (256, 128), 1)

    def shift(a):
        for b in range(6):
            mine = full[a, :, :, :, 128 * b : 128 * b + 128].reshape(256, 128).astype(F32)
            theirs = other[a, :, :, :, 128 * b : 128 * b + 128].reshape(256, 128).astype(F32)
            before = jnp.where(lane == 127, jnp.where(p == 1, theirs, 0.0), mine)
            after = jnp.where(lane == 0, jnp.where(p == 0, theirs, 0.0), mine)
            left[a, :, 128 * b : 128 * b + 128] = pltpu.roll(before, 1, 1).astype(BF16)
            right[a, :, 128 * b : 128 * b + 128] = pltpu.roll(after, 127, 1).astype(BF16)

    cot = full[1, :, :, :, 128:640].reshape(256, 512)
    core_in = []
    for s, dy in enumerate((1, 0, 2)):
        if s == 1:
            for copy in cross_v:
                copy.wait_recv()
            shift(0)
        for dx in range(3):
            r = lax.dot_general(window(0, dy, dx), cot, (((1,), (1,)), ((), ())), preferred_element_type=F32)
            kpart[9 * s + dx] = r[:128, 128:].reshape(4, 32, 128)
            kpart[9 * s + 3 + dx] = (r[:128, :128] + r[128:, 128:]).reshape(4, 32, 128)
            kpart[9 * s + 6 + dx] = r[128:, :128].reshape(4, 32, 128)
        span = pl.ds(9 * s, 9 if s < 2 else 10)
        core_in.append(push(kpart.at[span, :, their_half], kcore.at[span], at(tp=q)))

    def cross_taps():
        moves = []
        for copy, g in zip(tap_in, (x2, x1, x3)):
            copy.wait_recv()
            moves.append(push(taps.at[:, g, half], taps.at[:, g, half], at(tp=q)))
        return moves

    tap_core = cross_taps()

    for copy in core_in:
        copy.wait_recv()
    z_in = []
    for n, g in enumerate((z2, z1, z3)):
        span = pl.ds(7 * g, 7)
        total = (kcore[span] + kpart[span, :, half, :]).reshape(28, 16, 128)
        code, unit = encode(total)
        rsend[n, 0:28] = code
        rsend[n, 28] = unit
        z_in.append(push(rsend.at[n], rland.at[n], at(tz=g)))

    for copy in cot_edges:
        copy.wait_recv()
    cross_c = push(full.at[1], other.at[1], at(tp=q))

    def filt(dx, dy):
        t = dx * 3 + dy
        w0 = taps[t].reshape(128, 128)
        w1 = taps[9 + t].reshape(128, 128)
        w2 = taps[18 + t].reshape(128, 128)
        return jnp.concatenate([jnp.concatenate([w1, w0], 1), jnp.concatenate([w2, w1], 1)], 0)

    def first(a, h, to, g1, g2):
        cut = pl.ds(256 * h, 256)
        a0 = push(part.at[a, :, g1, :, cut], one.at[a, h, 0], to)
        a1 = push(part.at[a, :, g2, :, cut], one.at[a, h, 1], to)
        return a0, a1

    def response():
        acc = jnp.zeros((256, 512), F32)
        for dx in range(3):
            for dy in range(3):
                acc += lax.dot_general(
                    filt(dx, dy), window(0, dy, dx), (((0,), (0,)), ((), ())), preferred_element_type=F32
                )
        part[0] = acc.reshape(2, 4, 32, 512)
        return first(0, 0, at(ty=y3), y3, y2), first(0, 1, at(ty=y1), y1, y2)

    def volume_gradient():
        cross_c.wait_recv()
        shift(1)
        acc = jnp.zeros((256, 512), F32)
        for dx in range(3):
            for dy in range(3):
                acc += jnp.dot(filt(dx, dy), window(1, 2 - dy, 2 - dx), preferred_element_type=F32)
        part[1] = acc.reshape(2, 4, 32, 512)
        return first(1, 0, at(tx=x3), x3, x2), first(1, 1, at(tx=x1), x1, x2)

    def second(a, h, to, g, copies):
        for copy in copies:
            copy.wait_recv()
        one[a, h, 1] += part[a, :, g, :, 256 * h : 256 * h + 256]
        return push(one.at[a, h, 1], two.at[a, h], to)

    for copy in loads[2:]:
        copy.wait()
    for copy in tap_core:
        copy.wait_recv()
    aa, ab = response()
    ba, bb = volume_gradient()

    for copy in z_in:
        copy.wait_recv()
    mine = pl.ds(7 * z, 7)
    total = (kcore[mine] + kpart[mine, :, half, :]).reshape(28, 16, 128)
    for n in range(3):
        total = total + decode(rland[n, 0:28], rland[n, 28])
    total = (total * scale).reshape(7, 4, 16, 128)
    for g in range(4):
        code, unit = encode(total[:, g])
        fin[g, 0:7] = code
        fin[g, 7] = unit
    spread = {}
    for kz, gz in (("2", z2), ("1", z1), ("3", z3), ("0", z)):
        for kx, gx in (("2", x2), ("1", x1), ("3", x3), ("0", x)):
            if kz + kx != "00":
                there = kcode_ref.at[z, x, :, half, :]
                spread[kz + kx] = push(fin.at[gx], there, at(tx=gx, tz=gz))
    kcode_ref[z, x, :, half, :] = fin[pl.ds(x, 1)].reshape(8, 16, 128)


    def finish(a, g, out_ref, copies):
        for h, copy in enumerate(copies):
            copy.wait_recv()
            for d in range(2):
                total = part[a, d, pl.ds(g, 1), :, 256 * h : 256 * h + 256].reshape(32, 256) + one[a, h, 0, d] + two[a, h, d]
                for b in range(2):
                    rows32[a, pl.ds(d * 4 + 2 * h + b, 32, stride=8), :] = total[:, 128 * b : 128 * b + 128]
        out_ref[...] = rows32[a].astype(BF16)

    aa2, ab2 = second(0, 0, at(ty=y1), y1, aa), second(0, 1, at(ty=y3), y3, ab)
    ba2, bb2 = second(1, 0, at(tx=x1), x1, ba), second(1, 1, at(tx=x3), x3, bb)

    def hand_on(kz, gz):
        for kx in "0132":
            if kz + kx != "00":
                spread[kz + kx].wait_recv()
        return push(kcode_ref.at[gz, :, :, half, :], kcode_ref.at[gz, :, :, half, :], at(tp=q))

    k_in = [hand_on("0", z)]
    k_in += [hand_on("1", z1), hand_on("3", z3)]
    finish(0, y, resp_ref, (aa2, ab2))
    finish(1, x, vgrad_ref, (ba2, bb2))
    k_in.append(hand_on("2", z2))
    for copy in k_in:
        copy.wait_recv()
    for copy in sends:
        copy.wait_send()


def write(resp_ref, vgrad_ref, kcode_ref, resp_out, vgrad_out, kgrad_out, wide, sem):
    copies = [
        pltpu.make_async_copy(resp_ref, resp_out, sem.at[27]),
        pltpu.make_async_copy(vgrad_ref, vgrad_out, sem.at[28]),
    ]
    for copy in copies:
        copy.start()
    for n, (dz, dx, dy) in enumerate(ORDER):
        t = dz * 9 + dx * 3 + dy
        for g in range(4):
            code = kcode_ref[n // 7, g, n % 7].astype(F32)
            unit = kcode_ref[n // 7, g, 7].astype(F32) * (1.0 / SPAN)
            wide[t, :, 128 * g : 128 * g + 128] = jnp.log(code) * unit
        copy = pltpu.make_async_copy(wide.at[t], kgrad_out.at[t], sem.at[n])
        copy.start()
        copies.append(copy)
    for copy in copies:
        copy.wait()


def shards(volume, kernel, cotangent):
    cells = 2 * 16 * 256
    scale = 1.0 / float(cells) ** 0.5
    vmem = pl.BlockSpec(memory_space=pltpu.VMEM)
    hbm = pl.BlockSpec(memory_space=pl.ANY)
    operands = (volume.reshape(256, 128), cotangent.reshape(256, 128), kernel)
    resp, vgrad, kcode = pl.pallas_call(
        functools.partial(body, scale),
        out_shape=(
            jax.ShapeDtypeStruct((256, 128), BF16),
            jax.ShapeDtypeStruct((256, 128), BF16),
            jax.ShapeDtypeStruct((4, 4, 8, 32, 128), BF16),
        ),
        in_specs=[hbm, hbm, hbm],
        out_specs=(vmem, vmem, vmem),
        scratch_shapes=[
            pltpu.VMEM((2, 256, 128), BF16),
            pltpu.VMEM((2, 256, 128), F32),
            pltpu.VMEM((2, 2, 4, 32, 768), BF16),
            pltpu.VMEM((2, 2, 4, 32, 768), BF16),
            pltpu.VMEM((2, 256, 768), BF16),
            pltpu.VMEM((2, 256, 768), BF16),
            pltpu.VMEM((27, 4, 32, 128), BF16),
            pltpu.VMEM((28, 4, 32, 128), F32),
            pltpu.VMEM((28, 4, 16, 128), F32),
            pltpu.VMEM((3, 29, 16, 128), BF16),
            pltpu.VMEM((3, 29, 16, 128), BF16),
            pltpu.VMEM((4, 8, 16, 128), BF16),
            pltpu.VMEM((2, 2, 4, 32, 512), F32),
            pltpu.VMEM((2, 2, 2, 2, 32, 256), F32),
            pltpu.VMEM((2, 2, 2, 32, 256), F32),
            pltpu.SemaphoreType.DMA((80,)),
            pltpu.SemaphoreType.DMA((80,)),
            pltpu.SemaphoreType.DMA((3,)),
        ],
        compiler_params=pltpu.CompilerParams(
            collective_id=0, has_side_effects=True, vmem_limit_bytes=40 * 1024 * 1024
        ),
    )(*(pltpu.with_memory_space_constraint(a, pltpu.HBM) for a in operands))
    resp, vgrad, kgrad = pl.pallas_call(
        write,
        out_shape=(
            jax.ShapeDtypeStruct((256, 128), BF16),
            jax.ShapeDtypeStruct((256, 128), BF16),
            jax.ShapeDtypeStruct((27, 32, 512), F32),
        ),
        in_specs=[vmem, vmem, vmem],
        out_specs=(hbm, hbm, hbm),
        scratch_shapes=[pltpu.VMEM((27, 32, 512), F32), pltpu.SemaphoreType.DMA((29,))],
        compiler_params=pltpu.CompilerParams(vmem_limit_bytes=40 * 1024 * 1024),
    )(resp, vgrad, kcode)
    return (resp.reshape(volume.shape), vgrad.reshape(volume.shape), kgrad)


def solution(mesh):
    in_specs = (P("ch", None, "sx", "sy"), P(None, "ch", None), P("ch", None, "sx", "sy"))
    out_specs = (P("ch", None, "sx", "sy"), P("ch", None, "sx", "sy"), P(None, "ch", None))
    return jax.shard_map(shards, mesh=mesh, in_specs=in_specs, out_specs=out_specs, check_vma=False)
```

time: 49.6 us -> 39.6 us (0.80)
  Pallas kernels: 48.8 us -> 38.8 us
    pallas_call x1, Pallas kernels: 46.1 us -> 37.4 us  [shards(): pl.pallas_call(functools.partial(body, scale), out_shape=(jax.ShapeDtypeS...]
    pallas_call x1, Pallas kernels: 2.69 us -> 1.48 us  [shards(): pl.pallas_call(write, out_shape=(jax.ShapeDtypeStruct((256, 128), BF16),...]
where the time goes in v3:
time: 39.6 us; the launch traced here: 39.5 us
  Pallas kernels  38.8 us (98%)
  between operations  0.64 us (2%)
    pallas_call x1, Pallas kernels, shards(): pl.pallas_call(functools.partial(body, scale), out_shape=(jax.ShapeDtypeS...  37.4 us
    pallas_call x1, Pallas kernels, shards(): pl.pallas_call(write, out_shape=(jax.ShapeDtypeStruct((256, 128), BF16),...  1.48 us

profile of v3, /device:TPU:1, one launch (start us, length us, event | category | flops | bytes accessed | tf_op | source)
XLA Modules:
  0.0 39.5 jit_solution(3044667443772454718)
XLA Ops:
  0.6 37.4 %shard_map.58 = (bf16[256,128]{1,0:T(8,128)(2,1)S(1)}, bf16[256,128]{1,0:T(8,128)(2,1)S(1)}, bf16[4,4,8,32,128]{4,3,2,1,0:T(8,128)(2,1)S(1)}) custom-call(bf16[256,128]{1,0:T(8,128)(2,1)} %bitcast.4, bf16[256,128]{1,0:T(8,128)(2,1)} %bitcast.5, bf16[27,32,512]{2,1,0:T(8,128)(2,1)} %k_ref.1), custom_call_target="tpu_custom_call" | custom-call | tf_op jit(solution)/shard_map/pallas_call | solution.py:336
  38.0 1.5 %shard_map.59 = (bf16[256,128]{1,0:T(8,128)(2,1)}, bf16[256,128]{1,0:T(8,128)(2,1)}, f32[27,32,512]{2,1,0:T(8,128)}) custom-call(bf16[256,128]{1,0:T(8,128)(2,1)S(1)} %get-tuple-element.9.resp_ref, bf16[256,128]{1,0:T(8,128)(2,1)S(1)} %get-tuple-element.10.vgrad_ref, bf16[4,4,8,32,128]{4,3,2,1,0:T(8,128)(2,1)S(1)} %get-tuple-element.11.kcode_ref), custom_call_target="tpu_custom_call" | custom-call | tf_op jit(solution)/shard_map/pallas_call | solution.py:369

commit v4 on v3

--- a/solution.py
+++ b/solution.py
@@ -50,7 +50,7 @@
 
 def body(
     scale, v_ref, c_ref, k_ref, resp_ref, vgrad_ref, kcode_ref,
-    bricks, rows32, full, other, left, right, taps, kpart, kcore, rsend, rland, fin,
+    bricks, rows32, full, other, left, right, taps, far_left, far_right, sums, rsend, rland,
     part, one, two, send_sem, recv_sem, load_sem,
 ):
     c = lax.axis_index("ch")
@@ -68,12 +68,6 @@
         ty = y if ty is None else ty
         return {"ch": tx * 4 + ty, "sx": z if tz is None else tz, "sy": p if tp is None else tp}
 
-    partners = [at(tx=a, tz=b) for a in (x2, x1, x3, x) for b in (z2, z1, z3, z)][:-1]
-    partners += [at(ty=y2), at(ty=y1), at(ty=y3), at(tp=q)]
-    barrier = pltpu.get_barrier_semaphore()
-    for who in partners:
-        pl.semaphore_signal(barrier, inc=1, device_id=who, device_id_type=MESH)
-
     half = pl.ds(pl.multiple_of(16 * p, 16), 16)
     their_half = pl.ds(pl.multiple_of(16 * q, 16), 16)
     loads = [
@@ -86,6 +80,12 @@
     for copy in loads:
         copy.start()
 
+    partners = [at(tx=a, tz=b) for a in (x2, x1, x3, x) for b in (z2, z1, z3, z)][:-1]
+    partners += [at(ty=y2), at(ty=y1), at(ty=y3), at(tp=q)]
+    barrier = pltpu.get_barrier_semaphore()
+    for who in partners:
+        pl.semaphore_signal(barrier, inc=1, device_id=who, device_id_type=MESH)
+
     @pl.when(z == 0)
     def _():
         full[:, :, :, :, 0:128] = jnp.zeros((2, 2, 4, 32, 128), BF16)
@@ -94,7 +94,7 @@
     def _():
         full[:, :, :, :, 640:768] = jnp.zeros((2, 2, 4, 32, 128), BF16)
 
-    kpart[27] = jnp.zeros((4, 32, 128), F32)
+    sums[27] = jnp.zeros((4, 16, 128), F32)
 
     for a, g in ((0, x), (1, y)):
         loads[a].wait()
@@ -130,7 +130,7 @@
         ]
         if k != "0":
             vol_in[k].append(push(cells(0, x, 1, 4), cells(0, x, 1, 4), at(tx=g)))
-    cot_in = [push(cells(1, y, 1, 4), cells(1, y, 1, 4), at(ty=g)) for g in (y2, y1, y3)]
+    cot_in = [push(cells(1, y, 1, 4), cells(1, y, 1, 4), at(ty=g)) for g in (y1, y3, y2)]
 
     def send_taps():
         return [
@@ -138,55 +138,101 @@
             for g in (x2, x1, x3)
         ]
 
+
+    cross_v = {}
+
+    def arrive(k, g):
+        for copy in vol_in[k]:
+            copy.wait_recv()
+        cross_v[k] = push(full.at[0, :, g], other.at[0, :, g], at(tp=q))
+
+    cross_c = [push(cells(1, y, 1, 4), other.at[1, :, y, :, pl.ds(128, 512)], at(tp=q))]
+    arrive("0", x)
+    arrive("1", x1)
     tap_in = send_taps()
-
-    cross_v = []
-    for k, g in (("0", x), ("1", x1), ("3", x3), ("2", x2)):
-        for copy in vol_in[k]:
-            copy.wait_recv()
-        cross_v.append(push(full.at[0, :, g], other.at[0, :, g], at(tp=q)))
-    for copy in cot_in:
+    for copy, g in zip(cot_in, (y1, y3, y2)):
         copy.wait_recv()
+        cross_c.append(push(cells(1, g, 1, 4), other.at[1, :, g, :, pl.ds(128, 512)], at(tp=q)))
+    arrive("3", x3)
+    arrive("2", x2)
     every = pl.ds(0, 4)
+    low, high = pl.ds(0, 128), pl.ds(640, 128)
     cot_edges = [
-        push(
-            full.at[1, :, every, :, pl.ds(512, 128)], full.at[1, :, every, :, pl.ds(0, 128)], at(tz=up), z < 3, z > 0
-        ),
-        push(
-            full.at[1, :, every, :, pl.ds(128, 128)], full.at[1, :, every, :, pl.ds(640, 128)], at(tz=down), z > 0, z < 3
-        ),
+        push(full.at[1, :, every, :, pl.ds(512, 128)], full.at[1, :, every, :, low], at(tz=up), z < 3, z > 0),
+        push(full.at[1, :, every, :, pl.ds(128, 128)], full.at[1, :, every, :, high], at(tz=down), z > 0, z < 3),
     ]
 
     def window(a, dy, dx):
-        if dy == 1:
-            return full[a, :, :, :, 128 * dx : 128 * dx + 512].reshape(256, 512)
-        return (left if dy == 0 else right)[a, :, 128 * dx : 128 * dx + 512]
-
-    lane = lax.broadcasted_iota(jnp.int32, (256, 128), 1)
-
-    def shift(a):
+        ref = full if dy == 1 else left if dy == 0 else right
+        return ref[a, :, :, :, 128 * dx : 128 * dx + 512].reshape(256, 512)
+
+    def shift(near, far, side, place):
         for b in range(6):
-            mine = full[a, :, :, :, 128 * b : 128 * b + 128].reshape(256, 128).astype(F32)
-            theirs = other[a, :, :, :, 128 * b : 128 * b + 128].reshape(256, 128).astype(F32)
-            before = jnp.where(lane == 127, jnp.where(p == 1, theirs, 0.0), mine)
-            after = jnp.where(lane == 0, jnp.where(p == 0, theirs, 0.0), mine)
-            left[a, :, 128 * b : 128 * b + 128] = pltpu.roll(before, 1, 1).astype(BF16)
-            right[a, :, 128 * b : 128 * b + 128] = pltpu.roll(after, 127, 1).astype(BF16)
-
-    cot = full[1, :, :, :, 128:640].reshape(256, 512)
-    core_in = []
-    for s, dy in enumerate((1, 0, 2)):
-        if s == 1:
-            for copy in cross_v:
-                copy.wait_recv()
-            shift(0)
-        for dx in range(3):
-            r = lax.dot_general(window(0, dy, dx), cot, (((1,), (1,)), ((), ())), preferred_element_type=F32)
-            kpart[9 * s + dx] = r[:128, 128:].reshape(4, 32, 128)
-            kpart[9 * s + 3 + dx] = (r[:128, :128] + r[128:, 128:]).reshape(4, 32, 128)
-            kpart[9 * s + 6 + dx] = r[128:, :128].reshape(4, 32, 128)
-        span = pl.ds(9 * s, 9 if s < 2 else 10)
-        core_in.append(push(kpart.at[span, :, their_half], kcore.at[span], at(tp=q)))
+            mine = near[:, place[0], place[1], 128 * b : 128 * b + 128].astype(F32)
+            theirs = far[:, place[0], place[1], 128 * b : 128 * b + 128].astype(F32)
+            lane = lax.broadcasted_iota(jnp.int32, mine.shape, 3)
+            before = jnp.where(lane == 127, jnp.where(side == 1, theirs, 0.0), mine)
+            after = jnp.where(lane == 0, jnp.where(side == 0, theirs, 0.0), mine)
+            flat = (mine.size // 128, 128)
+            before = pltpu.roll(before.reshape(flat), 1, 1).astype(BF16).reshape(mine.shape)
+            after = pltpu.roll(after.reshape(flat), 127, 1).astype(BF16).reshape(mine.shape)
+            yield b, before, after
+
+    bases = (2 * (x // 2), 2 * (1 - x // 2))
+
+    def brick_gradient(h):
+        pair = pl.ds(bases[h], 2)
+        for b, before, after in shift(full.at[0], other.at[0], p, (pair, half)):
+            left[0, :, pair, half, 128 * b : 128 * b + 128] = before
+            right[0, :, pair, half, 128 * b : 128 * b + 128] = after
+        for b, before, after in shift(other.at[0], full.at[0], q, (pair, half)):
+            far_left[:, :, :, 128 * b : 128 * b + 128] = before
+            far_right[:, :, :, 128 * b : 128 * b + 128] = after
+        total = None
+        for refs, cots in (
+            ((full.at[0, :, pair, half], left.at[0, :, pair, half], right.at[0, :, pair, half]), full),
+            ((other.at[0, :, pair, half], far_left, far_right), other),
+        ):
+            cot = cots[1, :, :, :, 128:640].reshape(256, 512)
+            stack = [
+                refs[at_y][:, :, :, 128 * dx : 128 * dx + 512].reshape(64, 512) for at_y in range(3) for dx in range(3)
+            ]
+            r = lax.dot_general(
+                jnp.concatenate(stack, 0), cot, (((1,), (1,)), ((), ())), preferred_element_type=F32
+            )
+            total = r if total is None else total + r
+        for s in range(3):
+            for dx in range(3):
+                r = total[64 * (3 * s + dx) : 64 * (3 * s + dx) + 64]
+                sums[9 * s + dx, pair] = r[:32, 128:].reshape(2, 16, 128)
+                sums[9 * s + 3 + dx, pair] = (r[:32, :128] + r[32:, 128:]).reshape(2, 16, 128)
+                sums[9 * s + 6 + dx, pair] = r[32:, :128].reshape(2, 16, 128)
+
+    x_places = ((("1", x1), ("0", x)), (("2", x2), ("3", x3)))
+    z_places = (("2", z2), ("1", z1), ("3", z3), ("0", z))
+    z_in = ({}, {})
+
+    def send_sums(h):
+        pair = pl.ds(bases[h], 2)
+        for n, (kz, gz) in enumerate(z_places):
+            code, unit = encode(sums[pl.ds(7 * gz, 7), pair])
+            for g in range(2):
+                rsend[h, n, g, 0:7] = code[:, g]
+                rsend[h, n, g, 7] = unit[g]
+            for m, (kx, gx) in enumerate(x_places[h]):
+                if kz + kx != "00":
+                    z_in[h][kz + kx] = push(rsend.at[h, n, gx % 2], rland.at[h, n, m], at(tx=gx, tz=gz))
+
+    for copy in cross_c:
+        copy.wait_recv()
+    cross_v["0"].wait_recv()
+    cross_v["1"].wait_recv()
+    brick_gradient(0)
+    send_sums(0)
+    cross_v["3"].wait_recv()
+    cross_v["2"].wait_recv()
+    brick_gradient(1)
+    send_sums(1)
 
     def cross_taps():
         moves = []
@@ -197,20 +243,9 @@
 
     tap_core = cross_taps()
 
-    for copy in core_in:
-        copy.wait_recv()
-    z_in = []
-    for n, g in enumerate((z2, z1, z3)):
-        span = pl.ds(7 * g, 7)
-        total = (kcore[span] + kpart[span, :, half, :]).reshape(28, 16, 128)
-        code, unit = encode(total)
-        rsend[n, 0:28] = code
-        rsend[n, 28] = unit
-        z_in.append(push(rsend.at[n], rland.at[n], at(tz=g)))
-
     for copy in cot_edges:
         copy.wait_recv()
-    cross_c = push(full.at[1], other.at[1], at(tp=q))
+    cross_e = [push(full.at[1, :, every, :, side], other.at[1, :, every, :, side], at(tp=q)) for side in (low, high)]
 
     def filt(dx, dy):
         t = dx * 3 + dy
@@ -226,6 +261,9 @@
         return a0, a1
 
     def response():
+        for b, before, after in shift(full.at[0], other.at[0], p, (every, their_half)):
+            left[0, :, :, their_half, 128 * b : 128 * b + 128] = before
+            right[0, :, :, their_half, 128 * b : 128 * b + 128] = after
         acc = jnp.zeros((256, 512), F32)
         for dx in range(3):
             for dy in range(3):
@@ -236,8 +274,11 @@
         return first(0, 0, at(ty=y3), y3, y2), first(0, 1, at(ty=y1), y1, y2)
 
     def volume_gradient():
-        cross_c.wait_recv()
-        shift(1)
+        for copy in cross_e:
+            copy.wait_recv()
+        for b, before, after in shift(full.at[1], other.at[1], p, (every, pl.ds(0, 32))):
+            left[1, :, :, :, 128 * b : 128 * b + 128] = before
+            right[1, :, :, :, 128 * b : 128 * b + 128] = after
         acc = jnp.zeros((256, 512), F32)
         for dx in range(3):
             for dy in range(3):
@@ -258,25 +299,31 @@
     aa, ab = response()
     ba, bb = volume_gradient()
 
-    for copy in z_in:
-        copy.wait_recv()
     mine = pl.ds(7 * z, 7)
-    total = (kcore[mine] + kpart[mine, :, half, :]).reshape(28, 16, 128)
-    for n in range(3):
-        total = total + decode(rland[n, 0:28], rland[n, 28])
-    total = (total * scale).reshape(7, 4, 16, 128)
-    for g in range(4):
-        code, unit = encode(total[:, g])
-        fin[g, 0:7] = code
-        fin[g, 7] = unit
-    spread = {}
-    for kz, gz in (("2", z2), ("1", z1), ("3", z3), ("0", z)):
-        for kx, gx in (("2", x2), ("1", x1), ("3", x3), ("0", x)):
-            if kz + kx != "00":
-                there = kcode_ref.at[z, x, :, half, :]
-                spread[kz + kx] = push(fin.at[gx], there, at(tx=gx, tz=gz))
-    kcode_ref[z, x, :, half, :] = fin[pl.ds(x, 1)].reshape(8, 16, 128)
-
+    k_z, k_in = ({}, {}), []
+
+    def send_result(h):
+        for copy in z_in[h].values():
+            copy.wait_recv()
+        for m, (kx, gx) in enumerate(x_places[h]):
+            total = jnp.zeros((7, 16, 128), F32)
+            for n, (kz, gz) in enumerate(z_places):
+                if kz + kx == "00":
+                    total = total + sums[mine, pl.ds(x, 1)].reshape(7, 16, 128)
+                else:
+                    total = total + decode(rland[h, n, m, 0:7], rland[h, n, m, 7])
+            code, unit = encode(total * scale)
+            kcode_ref[z, gx, 0:7, half, :] = code
+            kcode_ref[z, gx, 7, half, :] = unit
+        there = kcode_ref.at[z, pl.ds(bases[h], 2), :, half, :]
+        for kz, gz in z_places[:3]:
+            k_z[h][kz] = push(there, there, at(tz=gz))
+        k_in.append(push(there, there, at(tp=q)))
+
+    send_result(0)
+    send_result(1)
+    aa2, ab2 = second(0, 0, at(ty=y1), y1, aa), second(0, 1, at(ty=y3), y3, ab)
+    ba2, bb2 = second(1, 0, at(tx=x1), x1, ba), second(1, 1, at(tx=x3), x3, bb)
 
     def finish(a, g, out_ref, copies):
         for h, copy in enumerate(copies):
@@ -287,20 +334,19 @@
                     rows32[a, pl.ds(d * 4 + 2 * h + b, 32, stride=8), :] = total[:, 128 * b : 128 * b + 128]
         out_ref[...] = rows32[a].astype(BF16)
 
-    aa2, ab2 = second(0, 0, at(ty=y1), y1, aa), second(0, 1, at(ty=y3), y3, ab)
-    ba2, bb2 = second(1, 0, at(tx=x1), x1, ba), second(1, 1, at(tx=x3), x3, bb)
-
-    def hand_on(kz, gz):
-        for kx in "0132":
-            if kz + kx != "00":
-                spread[kz + kx].wait_recv()
-        return push(kcode_ref.at[gz, :, :, half, :], kcode_ref.at[gz, :, :, half, :], at(tp=q))
-
-    k_in = [hand_on("0", z)]
-    k_in += [hand_on("1", z1), hand_on("3", z3)]
+
+    def hand_on(h, kz, gz):
+        k_z[h][kz].wait_recv()
+        there = kcode_ref.at[gz, pl.ds(bases[h], 2), :, half, :]
+        k_in.append(push(there, there, at(tp=q)))
+
+    for h, kz, gz in ((0, "1", z1), (0, "3", z3), (0, "2", z2)):
+        hand_on(h, kz, gz)
+    hand_on(1, "1", z1)
+    hand_on(1, "3", z3)
     finish(0, y, resp_ref, (aa2, ab2))
     finish(1, x, vgrad_ref, (ba2, bb2))
-    k_in.append(hand_on("2", z2))
+    hand_on(1, "2", z2)
     for copy in k_in:
         copy.wait_recv()
     for copy in sends:
@@ -347,14 +393,14 @@
             pltpu.VMEM((2, 256, 128), F32),
             pltpu.VMEM((2, 2, 4, 32, 768), BF16),
             pltpu.VMEM((2, 2, 4, 32, 768), BF16),
-            pltpu.VMEM((2, 256, 768), BF16),
-            pltpu.VMEM((2, 256, 768), BF16),
+            pltpu.VMEM((2, 2, 4, 32, 768), BF16),
+            pltpu.VMEM((2, 2, 4, 32, 768), BF16),
             pltpu.VMEM((27, 4, 32, 128), BF16),
-            pltpu.VMEM((28, 4, 32, 128), F32),
+            pltpu.VMEM((2, 2, 16, 768), BF16),
+            pltpu.VMEM((2, 2, 16, 768), BF16),
             pltpu.VMEM((28, 4, 16, 128), F32),
-            pltpu.VMEM((3, 29, 16, 128), BF16),
-            pltpu.VMEM((3, 29, 16, 128), BF16),
-            pltpu.VMEM((4, 8, 16, 128), BF16),
+            pltpu.VMEM((2, 4, 2, 8, 16, 128), BF16),
+            pltpu.VMEM((2, 4, 2, 8, 16, 128), BF16),
             pltpu.VMEM((2, 2, 4, 32, 512), F32),
             pltpu.VMEM((2, 2, 2, 2, 32, 256), F32),
             pltpu.VMEM((2, 2, 2, 32, 256), F32),

time: 39.6 us -> 37 us (0.934)
  Pallas kernels: 38.8 us -> 36.2 us
    pallas_call x1, Pallas kernels: 37.4 us -> 34.7 us  [shards(): pl.pallas_call(functools.partial(body, scale), out_shape=(jax.ShapeDtypeS...]
where the time goes in v4:
time: 37 us; the launch traced here: 36.8 us
  Pallas kernels  36.2 us (98%)
  between operations  0.64 us (2%)
    pallas_call x1, Pallas kernels, shards(): pl.pallas_call(functools.partial(body, scale), out_shape=(jax.ShapeDtypeS...  34.7 us
    pallas_call x1, Pallas kernels, shards(): pl.pallas_call(write, out_shape=(jax.ShapeDtypeStruct((256, 128), BF16),...  1.48 us

profile of v4, /device:TPU:1, one launch (start us, length us, event | category | flops | bytes accessed | tf_op | source)
XLA Modules:
  0.0 36.8 jit_solution(18194660129726631214)
XLA Ops:
  0.6 34.7 %shard_map.58 = (bf16[256,128]{1,0:T(8,128)(2,1)S(1)}, bf16[256,128]{1,0:T(8,128)(2,1)S(1)}, bf16[4,4,8,32,128]{4,3,2,1,0:T(8,128)(2,1)S(1)}) custom-call(bf16[256,128]{1,0:T(8,128)(2,1)} %bitcast.4, bf16[256,128]{1,0:T(8,128)(2,1)} %bitcast.5, bf16[27,32,512]{2,1,0:T(8,128)(2,1)} %k_ref.1), custom_call_target="tpu_custom_call" | custom-call | tf_op jit(solution)/shard_map/pallas_call | solution.py:382
  35.4 1.5 %shard_map.59 = (bf16[256,128]{1,0:T(8,128)(2,1)}, bf16[256,128]{1,0:T(8,128)(2,1)}, f32[27,32,512]{2,1,0:T(8,128)}) custom-call(bf16[256,128]{1,0:T(8,128)(2,1)S(1)} %get-tuple-element.9.resp_ref, bf16[256,128]{1,0:T(8,128)(2,1)S(1)} %get-tuple-element.10.vgrad_ref, bf16[4,4,8,32,128]{4,3,2,1,0:T(8,128)(2,1)S(1)} %get-tuple-element.11.kcode_ref), custom_call_target="tpu_custom_call" | custom-call | tf_op jit(solution)/shard_map/pallas_call | solution.py:415

commit v5 on v4

--- a/solution.py
+++ b/solution.py
@@ -11,7 +11,6 @@
 F32 = jnp.float32
 BF16 = jnp.bfloat16
 SPAN = 86.0
-ORDER = [(dz, dx, dy) for dy in (1, 0, 2) for dz in range(3) for dx in range(3)]
 
 
 def nearby(i):
@@ -118,6 +117,11 @@
         move = Move(copy, may_send, may_recv)
         sends.append(move)
         return move
+
+    def drain(upto):
+        for move in sends[:upto]:
+            move.wait_send()
+        del sends[:upto]
 
     def cells(a, g, first, n):
         return full.at[a, :, g, :, pl.ds(128 * first, 128 * n)]
@@ -170,7 +174,7 @@
         for b in range(6):
             mine = near[:, place[0], place[1], 128 * b : 128 * b + 128].astype(F32)
             theirs = far[:, place[0], place[1], 128 * b : 128 * b + 128].astype(F32)
-            lane = lax.broadcasted_iota(jnp.int32, mine.shape, 3)
+            lane = lax.broadcasted_iota(jnp.int32, mine.shape, mine.ndim - 1)
             before = jnp.where(lane == 127, jnp.where(side == 1, theirs, 0.0), mine)
             after = jnp.where(lane == 0, jnp.where(side == 0, theirs, 0.0), mine)
             flat = (mine.size // 128, 128)
@@ -178,24 +182,28 @@
             after = pltpu.roll(after.reshape(flat), 127, 1).astype(BF16).reshape(mine.shape)
             yield b, before, after
 
-    bases = (2 * (x // 2), 2 * (1 - x // 2))
+    x_places = ((("0", x), ("1", x1)), (("3", x3), ("2", x2)))
+    z_places = (("2", z2), ("1", z1), ("3", z3), ("0", z))
 
     def brick_gradient(h):
-        pair = pl.ds(bases[h], 2)
-        for b, before, after in shift(full.at[0], other.at[0], p, (pair, half)):
-            left[0, :, pair, half, 128 * b : 128 * b + 128] = before
-            right[0, :, pair, half, 128 * b : 128 * b + 128] = after
-        for b, before, after in shift(other.at[0], full.at[0], q, (pair, half)):
-            far_left[:, :, :, 128 * b : 128 * b + 128] = before
-            far_right[:, :, :, 128 * b : 128 * b + 128] = after
         total = None
-        for refs, cots in (
-            ((full.at[0, :, pair, half], left.at[0, :, pair, half], right.at[0, :, pair, half]), full),
-            ((other.at[0, :, pair, half], far_left, far_right), other),
-        ):
+        views = []
+        for m, (kx, g) in enumerate(x_places[h]):
+            for b, before, after in shift(full.at[0], other.at[0], p, (g, half)):
+                left[0, :, g, half, 128 * b : 128 * b + 128] = before
+                right[0, :, g, half, 128 * b : 128 * b + 128] = after
+            for b, before, after in shift(other.at[0], full.at[0], q, (g, half)):
+                far_left[m, :, :, 128 * b : 128 * b + 128] = before
+                far_right[m, :, :, 128 * b : 128 * b + 128] = after
+            views.append((
+                (full.at[0, :, g, half], left.at[0, :, g, half], right.at[0, :, g, half]),
+                (other.at[0, :, g, half], far_left.at[m], far_right.at[m]),
+            ))
+        for brick, cots in ((0, full), (1, other)):
             cot = cots[1, :, :, :, 128:640].reshape(256, 512)
             stack = [
-                refs[at_y][:, :, :, 128 * dx : 128 * dx + 512].reshape(64, 512) for at_y in range(3) for dx in range(3)
+                views[m][brick][s][:, :, 128 * dx : 128 * dx + 512].reshape(32, 512)
+                for s in range(3) for dx in range(3) for m in range(2)
             ]
             r = lax.dot_general(
                 jnp.concatenate(stack, 0), cot, (((1,), (1,)), ((), ())), preferred_element_type=F32
@@ -203,36 +211,32 @@
             total = r if total is None else total + r
         for s in range(3):
             for dx in range(3):
-                r = total[64 * (3 * s + dx) : 64 * (3 * s + dx) + 64]
-                sums[9 * s + dx, pair] = r[:32, 128:].reshape(2, 16, 128)
-                sums[9 * s + 3 + dx, pair] = (r[:32, :128] + r[32:, 128:]).reshape(2, 16, 128)
-                sums[9 * s + 6 + dx, pair] = r[32:, :128].reshape(2, 16, 128)
-
-    x_places = ((("1", x1), ("0", x)), (("2", x2), ("3", x3)))
-    z_places = (("2", z2), ("1", z1), ("3", z3), ("0", z))
+                for m, (kx, g) in enumerate(x_places[h]):
+                    at_row = 32 * (6 * s + 2 * dx + m)
+                    r = total[at_row : at_row + 32]
+                    tap = 3 * dx + (1, 0, 2)[s]
+                    sums[tap, g] = r[:16, 128:]
+                    sums[9 + tap, g] = r[:16, :128] + r[16:, 128:]
+                    sums[18 + tap, g] = r[16:, :128]
+
     z_in = ({}, {})
 
     def send_sums(h):
-        pair = pl.ds(bases[h], 2)
         for n, (kz, gz) in enumerate(z_places):
-            code, unit = encode(sums[pl.ds(7 * gz, 7), pair])
-            for g in range(2):
-                rsend[h, n, g, 0:7] = code[:, g]
-                rsend[h, n, g, 7] = unit[g]
             for m, (kx, gx) in enumerate(x_places[h]):
                 if kz + kx != "00":
-                    z_in[h][kz + kx] = push(rsend.at[h, n, gx % 2], rland.at[h, n, m], at(tx=gx, tz=gz))
+                    code, unit = encode(sums[pl.ds(7 * gz, 7), pl.ds(gx, 1)].reshape(7, 16, 128))
+                    rsend[h, n, m, 0:7] = code
+                    rsend[h, n, m, 7] = unit
+                    z_in[h][kz + kx] = push(rsend.at[h, n, m], rland.at[h, n, m], at(tx=gx, tz=gz))
 
     for copy in cross_c:
         copy.wait_recv()
-    cross_v["0"].wait_recv()
-    cross_v["1"].wait_recv()
-    brick_gradient(0)
-    send_sums(0)
-    cross_v["3"].wait_recv()
-    cross_v["2"].wait_recv()
-    brick_gradient(1)
-    send_sums(1)
+    for h in range(2):
+        for kx, g in x_places[h]:
+            cross_v[kx].wait_recv()
+        brick_gradient(h)
+        send_sums(h)
 
     def cross_taps():
         moves = []
@@ -296,8 +300,10 @@
         copy.wait()
     for copy in tap_core:
         copy.wait_recv()
+    early = len(sends)
     aa, ab = response()
     ba, bb = volume_gradient()
+    drain(early)
 
     mine = pl.ds(7 * z, 7)
     k_z, k_in = ({}, {}), []
@@ -313,9 +319,9 @@
                 else:
                     total = total + decode(rland[h, n, m, 0:7], rland[h, n, m, 7])
             code, unit = encode(total * scale)
-            kcode_ref[z, gx, 0:7, half, :] = code
-            kcode_ref[z, gx, 7, half, :] = unit
-        there = kcode_ref.at[z, pl.ds(bases[h], 2), :, half, :]
+            kcode_ref[z, h, m, 0:7, half, :] = code
+            kcode_ref[z, h, m, 7, half, :] = unit
+        there = kcode_ref.at[z, h, :, :, half, :]
         for kz, gz in z_places[:3]:
             k_z[h][kz] = push(there, there, at(tz=gz))
         k_in.append(push(there, there, at(tp=q)))
@@ -335,9 +341,11 @@
         out_ref[...] = rows32[a].astype(BF16)
 
 
+    drain(len(sends) - 12)
+
     def hand_on(h, kz, gz):
         k_z[h][kz].wait_recv()
-        there = kcode_ref.at[gz, pl.ds(bases[h], 2), :, half, :]
+        there = kcode_ref.at[gz, h, :, :, half, :]
         k_in.append(push(there, there, at(tp=q)))
 
     for h, kz, gz in ((0, "1", z1), (0, "3", z3), (0, "2", z2)):
@@ -345,8 +353,8 @@
     hand_on(1, "1", z1)
     hand_on(1, "3", z3)
     finish(0, y, resp_ref, (aa2, ab2))
+    hand_on(1, "2", z2)
     finish(1, x, vgrad_ref, (ba2, bb2))
-    hand_on(1, "2", z2)
     for copy in k_in:
         copy.wait_recv()
     for copy in sends:
@@ -360,15 +368,18 @@
     ]
     for copy in copies:
         copy.start()
-    for n, (dz, dx, dy) in enumerate(ORDER):
-        t = dz * 9 + dx * 3 + dy
-        for g in range(4):
-            code = kcode_ref[n // 7, g, n % 7].astype(F32)
-            unit = kcode_ref[n // 7, g, 7].astype(F32) * (1.0 / SPAN)
-            wide[t, :, 128 * g : 128 * g + 128] = jnp.log(code) * unit
-        copy = pltpu.make_async_copy(wide.at[t], kgrad_out.at[t], sem.at[n])
-        copy.start()
-        copies.append(copy)
+    x = lax.axis_index("ch") // 4
+    x1, x3, x2 = nearby(x)
+    places = (x, x1, x3, x2)
+    for t in range(27):
+        for k, g in enumerate(places):
+            code = kcode_ref[t // 7, k // 2, k % 2, t % 7].astype(F32)
+            unit = kcode_ref[t // 7, k // 2, k % 2, 7].astype(F32) * (1.0 / SPAN)
+            wide[t, :, pl.ds(pl.multiple_of(128 * g, 128), 128)] = jnp.log(code) * unit
+        if t % 1 == 0:
+            span = pl.ds(t - 0, 1)
+            copies.append(pltpu.make_async_copy(wide.at[span], kgrad_out.at[span], sem.at[t]))
+            copies[-1].start()
     for copy in copies:
         copy.wait()
 
@@ -384,7 +395,7 @@
         out_shape=(
             jax.ShapeDtypeStruct((256, 128), BF16),
             jax.ShapeDtypeStruct((256, 128), BF16),
-            jax.ShapeDtypeStruct((4, 4, 8, 32, 128), BF16),
+            jax.ShapeDtypeStruct((4, 2, 2, 8, 32, 128), BF16),
         ),
         in_specs=[hbm, hbm, hbm],
         out_specs=(vmem, vmem, vmem),

time: 37 us -> 36.8 us (level)
  no operation moved by 1% of the time
where the time goes in v5:
time: 36.8 us; the launch traced here: 36.7 us
  Pallas kernels  36 us (98%)
  between operations  0.64 us (2%)
    pallas_call x1, Pallas kernels, shards(): pl.pallas_call(functools.partial(body, scale), out_shape=(jax.ShapeDtypeS...  34.6 us
    pallas_call x1, Pallas kernels, shards(): pl.pallas_call(write, out_shape=(jax.ShapeDtypeStruct((256, 128), BF16),...  1.48 us

profile of v5, /device:TPU:1, one launch (start us, length us, event | category | flops | bytes accessed | tf_op | source)
XLA Modules:
  0.0 36.7 jit_solution(8564927813489855353)
XLA Ops:
  0.6 34.6 %shard_map.58 = (bf16[256,128]{1,0:T(8,128)(2,1)S(1)}, bf16[256,128]{1,0:T(8,128)(2,1)S(1)}, bf16[4,2,2,8,32,128]{5,4,3,2,1,0:T(8,128)(2,1)S(1)}) custom-call(bf16[256,128]{1,0:T(8,128)(2,1)} %bitcast.4, bf16[256,128]{1,0:T(8,128)(2,1)} %bitcast.5, bf16[27,32,512]{2,1,0:T(8,128)(2,1)} %k_ref.1), custom_call_target="tpu_custom_call" | custom-call | tf_op jit(solution)/shard_map/pallas_call | solution.py:393
  35.2 1.5 %shard_map.59 = (bf16[256,128]{1,0:T(8,128)(2,1)}, bf16[256,128]{1,0:T(8,128)(2,1)}, f32[27,32,512]{2,1,0:T(8,128)}) custom-call(bf16[256,128]{1,0:T(8,128)(2,1)S(1)} %get-tuple-element.9.resp_ref, bf16[256,128]{1,0:T(8,128)(2,1)S(1)} %get-tuple-element.10.vgrad_ref, bf16[4,2,2,8,32,128]{5,4,3,2,1,0:T(8,128)(2,1)S(1)} %get-tuple-element.11.kcode_ref), custom_call_target="tpu_custom_call" | custom-call | tf_op jit(solution)/shard_map/pallas_call | solution.py:426
